TPU v7x, 256 devices: a whole 4x4x8 slice. The times are simulated.
256 devices in a mesh: seq: 64 (over x, z, core), ep: 4 (over y).
Axes of the slice: x: 4, y: 4, z: 8, core: 2. Of those that a mesh axis runs over, the one named last changes fastest.
Arguments:
- queries: bfloat16 [8192, 4096], P('seq', 'ep'), may hold values from -256 to 256
- keys: bfloat16 [8192, 512], P('seq', 'ep'), may hold values from -6 to 6
- values: bfloat16 [8192, 512], P('seq', 'ep'), may hold values from -6 to 6
- hidden: bfloat16 [8192, 2048], P('seq'), may hold values from -6 to 6
- cotangent: bfloat16 [8192, 2048], P('seq'), may hold values from -6 to 6
- routes: int32 [8192, 8], P('seq'), may hold values from 0 to 31, all different within a row; in each aligned block of 128 rows (0 to 127, 128 to 255, ...) at most 40 rows name the same one
- route_weight: float32 [8192, 8], P('seq'), may hold values from 0.2 to 1
- w_gate_up: bfloat16 [4, 64, 2048, 384], P('ep', 'seq'), may hold values from -0.125 to 0.125
- w_down: bfloat16 [4, 64, 192, 2048], P('ep', 'seq'), may hold values from -0.15625 to 0.15625
- adapter_in: bfloat16 [4, 64, 2048, 16], P('ep', 'seq'), may hold values from -0.125 to 0.125
- adapter_out: bfloat16 [4, 64, 64, 384], P('ep', 'seq'), may hold values from -0.75 to 0.75
Outputs:
- context: bfloat16 [8192, 4096], P('seq', 'ep')
- mixed: bfloat16 [8192, 2048], P('seq', 'ep')
- grad_adapter_in: float32 [4, 64, 2048, 16], P('ep', 'seq')
- grad_adapter_out: float32 [4, 64, 64, 384], P('ep', 'seq')
Inputs may be any that keep to these rules, and one draw needn't show every extreme that they name: `routes`: among the 128 tokens of each seq index at most 40 pick any one expert, and 40 is reached; a token's 8 experts differ.
All inputs are finite; a program needn't handle non-finite values.
Results may differ from a plain program's by a relative error of at most 0.017.
Values may be sent and summed in bfloat16 or wider, within the bound.
A program may use at most 128 MiB of HBM per device.

v0:
```python
import math

import jax
import jax.numpy as jnp
import numpy as np
from jax import lax
from jax.sharding import PartitionSpec as P

HEAD_WIDTH = 128
EXPERTS = 32
CAP = 40


def from_partner(block, axis, distance):
    count = lax.axis_size(axis)
    route = []
    for low in range(count):
        high = low | 1 << distance
        if high != low and high < count:
            route += [(low, high), (high, low)]
    return lax.ppermute(block, axis, route)


def absorb_block(carry, key_block, value_block, offset, units, query_pos, scale):
    top_run, total_run, accum = carry
    key_pos = offset + jnp.arange(key_block.shape[0], dtype=jnp.int32)
    scores = jnp.einsum("uqd,nd->uqn", units, key_block, preferred_element_type=jnp.float32)
    allowed = key_pos[None, None, :] <= query_pos[:, :, None]
    masked = jnp.where(allowed, scores, -1e30)
    top_new = jnp.maximum(top_run, jnp.max(masked, axis=2))
    factor = jnp.exp((top_run - top_new) * scale)
    weights = jnp.exp((masked - top_new[:, :, None]) * scale)
    total_new = total_run * factor + jnp.sum(weights, axis=2)
    accum_new = accum * factor[:, :, None] + jnp.einsum(
        "uqn,nd->uqd", weights.astype(jnp.bfloat16), value_block, preferred_element_type=jnp.float32
    )
    return (top_new, total_new, accum_new)


def attend(queries, keys, values, seq_count, seq_index):
    tok_rows = queries.shape[0]
    head_count = queries.shape[1] // HEAD_WIDTH
    split_count = max(1, seq_count // head_count)
    unit_count = head_count * split_count // seq_count
    part_rows = tok_rows // split_count
    local_units = (
        queries.reshape(split_count, part_rows, head_count, HEAD_WIDTH)
        .transpose(2, 0, 1, 3)
        .reshape(head_count * split_count, part_rows, HEAD_WIDTH)
    )
    units = lax.all_to_all(local_units, "seq", split_axis=0, concat_axis=1, tiled=True)
    query_total = seq_count * part_rows
    unit_ids = seq_index * unit_count + jnp.arange(unit_count, dtype=jnp.int32)
    part_ids = unit_ids % split_count
    row_ids = jnp.arange(query_total, dtype=jnp.int32)
    query_pos = (
        (row_ids // part_rows)[None, :] * tok_rows
        + part_ids[:, None] * part_rows
        + (row_ids % part_rows)[None, :]
    )
    scale = HEAD_WIDTH ** (-0.5)
    start_state = (
        jnp.full((unit_count, query_total), -1e30, jnp.float32),
        jnp.zeros((unit_count, query_total), jnp.float32),
        jnp.zeros((unit_count, query_total, HEAD_WIDTH), jnp.float32),
    )
    key_piece = lax.all_gather(keys, "seq", axis=0, tiled=True)
    value_piece = lax.all_gather(values, "seq", axis=0, tiled=True)
    count = key_piece.shape[0]
    block = math.gcd(count, 1024)
    steps = count // block
    key_blocks = key_piece.reshape(steps, block, HEAD_WIDTH)
    value_blocks = value_piece.reshape(steps, block, HEAD_WIDTH)
    offsets = block * jnp.arange(steps, dtype=jnp.int32)

    def inner(state, item):
        key_block, value_block, offset = item
        return (absorb_block(state, key_block, value_block, offset, units, query_pos, scale), None)

    result, _ = lax.scan(inner, start_state, (key_blocks, value_blocks, offsets))
    top_run, total_run, accum = result
    result = (accum / total_run[:, :, None]).astype(jnp.bfloat16)
    returned = lax.all_to_all(result, "seq", split_axis=1, concat_axis=0, tiled=True)
    return (
        returned.reshape(head_count, split_count, part_rows, HEAD_WIDTH)
        .transpose(1, 2, 0, 3)
        .reshape(tok_rows, head_count * HEAD_WIDTH)
    )


def collect_parts(flat, bit_order):
    stack = flat[None]
    for level in bit_order:
        other = from_partner(stack, "seq", level)
        stack = jnp.concatenate([stack, other], axis=0)
    return stack


def unpack_parts(stack, shapes):
    result = []
    offset = 0
    for shape in shapes:
        count = math.prod(shape)
        result.append(stack[:, offset : offset + count].reshape((stack.shape[0],) + tuple(shape)))
        offset = offset + count
    return result


def reduce_parts(first, second, first_axes, second_axes, bit_order):
    for step, level in enumerate(bit_order):
        keep_first = lax.slice_in_dim(first, 0, 1, axis=first_axes[step])
        send_first = lax.slice_in_dim(first, 1, 2, axis=first_axes[step])
        keep_second = lax.slice_in_dim(second, 0, 1, axis=second_axes[step])
        send_second = lax.slice_in_dim(second, 1, 2, axis=second_axes[step])
        outgoing = jnp.concatenate([send_first.reshape(-1), send_second.reshape(-1)])
        incoming = from_partner(outgoing.astype(jnp.bfloat16), "seq", level).astype(outgoing.dtype)
        first_count = send_first.size
        first = keep_first + incoming[:first_count].reshape(keep_first.shape)
        second = keep_second + incoming[first_count:].reshape(keep_second.shape)
    return (first, second)


def local(
    queries,
    keys,
    values,
    hidden,
    cotangent,
    routes,
    route_weight,
    w_gate_up,
    w_down,
    adapter_in,
    adapter_out,
):
    seq_count = lax.axis_size("seq")
    seq_index = lax.axis_index("seq")
    ep_count = lax.axis_size("ep")
    ep_index = lax.axis_index("ep")
    context = attend(queries, keys, values, seq_count, seq_index)
    width = hidden.shape[1]
    experts_here = EXPERTS // ep_count
    group_size = seq_count * ep_count // EXPERTS
    level_list = group_size.bit_length() - 1
    slot_part = CAP // group_size
    bit_order = list(range(level_list))
    mask_table = np.zeros((group_size,), np.int32)
    inverse_table = np.zeros((group_size,), np.int32)
    for position in range(group_size):
        bits_value = 0
        for step, level in enumerate(bit_order):
            if position >> step & 1:
                bits_value = bits_value | 1 << level
        mask_table[position] = bits_value
        inverse_table[bits_value] = position
    own_part = seq_index % group_size
    part_of_position = jnp.bitwise_xor(own_part, jnp.asarray(mask_table))
    position_of_part = jnp.take(
        jnp.asarray(inverse_table),
        jnp.bitwise_xor(jnp.arange(group_size, dtype=jnp.int32), own_part),
    )
    local_ids = ep_index * experts_here + jnp.arange(experts_here, dtype=jnp.int32)
    picked = routes[:, :, None] == local_ids[None, None, :]
    chosen = jnp.sum(picked.astype(jnp.int32), axis=1)
    coef = jnp.sum(jnp.where(picked, route_weight[:, :, None], 0.0), axis=1)
    slot_ids = jnp.cumsum(chosen, axis=0) - chosen
    slot_range = jnp.arange(CAP, dtype=jnp.int32)
    onehot = (
        (slot_ids.T[:, None, :] == slot_range[None, :, None]) & (chosen.T[:, None, :] > 0)
    ).astype(jnp.float32)
    scaled_sel = onehot * coef.T[:, None, :]
    rows_out = jnp.einsum(
        "xct,td->xcd", onehot.astype(jnp.bfloat16), hidden, preferred_element_type=jnp.float32
    ).astype(jnp.bfloat16)
    grads_out = jnp.einsum(
        "xct,td->xcd", scaled_sel, cotangent.astype(jnp.float32), precision=lax.Precision.HIGHEST
    ).astype(jnp.bfloat16)
    send_rows = rows_out.reshape(seq_count, slot_part, width)
    send_grads = grads_out.reshape(seq_count, slot_part, width)
    recv_rows, recv_grads = (
        lax.all_to_all(send_rows, "seq", split_axis=0, concat_axis=0, tiled=True),
        lax.all_to_all(send_grads, "seq", split_axis=0, concat_axis=0, tiled=True),
    )
    row_count = seq_count * slot_part
    rows_in = recv_rows.reshape(row_count, width)
    grads_in = recv_grads.reshape(row_count, width)
    gate_up_w = w_gate_up[0, 0]
    down_w = w_down[0, 0]
    low_in = adapter_in[0, 0]
    low_out = adapter_out[0, 0]
    hidden_part = down_w.shape[0]
    half_units = hidden_part // 2
    rank_size = low_out.shape[0]
    low_cols = low_in.shape[1]
    out_rows = jnp.zeros((row_count, width), jnp.float32)
    grad_low_gate = jnp.zeros((row_count, rank_size), jnp.float32)
    grad_low_up = jnp.zeros((row_count, rank_size), jnp.float32)
    grad_gate_parts = []
    grad_up_parts = []
    for half in range(2):
        begin = half * half_units
        pieces = [
            gate_up_w[:, begin : begin + half_units],
            gate_up_w[:, hidden_part + begin : hidden_part + begin + half_units],
            down_w[begin : begin + half_units],
            low_out[:, begin : begin + half_units],
            low_out[:, hidden_part + begin : hidden_part + begin + half_units],
        ]
        if half == 0:
            pieces = pieces + [low_in]
        shapes = [piece.shape for piece in pieces]
        flat = jnp.concatenate([piece.reshape(-1) for piece in pieces])
        stack = collect_parts(flat, bit_order)
        parts = unpack_parts(stack, shapes)
        gate_cols, up_cols, down_rows, bg_cols, bu_cols = (
            parts[0],
            parts[1],
            parts[2],
            parts[3],
            parts[4],
        )
        if half == 0:
            low_pos = jnp.einsum(
                "rd,gdl->rgl", rows_in, parts[5], preferred_element_type=jnp.float32
            )
            low_true = jnp.take(low_pos, position_of_part, axis=1)
            low = low_true.reshape(row_count, 2 * rank_size).astype(jnp.bfloat16)
            low_gate = low[:, :rank_size]
            low_up = low[:, rank_size:]
        pre_gate = jnp.einsum(
            "rd,gdq->rgq", rows_in, gate_cols, preferred_element_type=jnp.float32
        ) + jnp.einsum("rk,gkq->rgq", low_gate, bg_cols, preferred_element_type=jnp.float32)
        pre_up = jnp.einsum(
            "rd,gdq->rgq", rows_in, up_cols, preferred_element_type=jnp.float32
        ) + jnp.einsum("rk,gkq->rgq", low_up, bu_cols, preferred_element_type=jnp.float32)
        active = (jax.nn.silu(pre_gate) * pre_up).astype(jnp.bfloat16)
        out_rows = out_rows + jnp.einsum(
            "rgq,gqd->rd", active, down_rows, preferred_element_type=jnp.float32
        )
        back_act = jnp.einsum(
            "rd,gqd->rgq", grads_in, down_rows, preferred_element_type=jnp.float32
        )
        sigmoid_val = jax.nn.sigmoid(pre_gate)
        grad_gate = (
            back_act * pre_up * sigmoid_val * (1.0 + pre_gate * (1.0 - sigmoid_val))
        ).astype(jnp.bfloat16)
        grad_up = (back_act * jax.nn.silu(pre_gate)).astype(jnp.bfloat16)
        grad_gate_parts.append(
            jnp.einsum("rk,rgq->gkq", low_gate, grad_gate, preferred_element_type=jnp.float32)
        )
        grad_up_parts.append(
            jnp.einsum("rk,rgq->gkq", low_up, grad_up, preferred_element_type=jnp.float32)
        )
        grad_low_gate = grad_low_gate + jnp.einsum(
            "rgq,gkq->rk", grad_gate, bg_cols, preferred_element_type=jnp.float32
        )
        grad_low_up = grad_low_up + jnp.einsum(
            "rgq,gkq->rk", grad_up, bu_cols, preferred_element_type=jnp.float32
        )
    grad_low = jnp.concatenate([grad_low_gate, grad_low_up], axis=1).astype(jnp.bfloat16)
    grad_low_stack = jnp.take(
        grad_low.reshape(row_count, group_size, low_cols), part_of_position, axis=1
    ).reshape(row_count, group_size * low_cols)
    grad_in_full = lax.dot_general(
        rows_in, grad_low_stack, (((0,), (0,)), ((), ())), preferred_element_type=jnp.float32
    )
    grad_out_full = jnp.concatenate(
        [grad_gate_parts[0], grad_gate_parts[1], grad_up_parts[0], grad_up_parts[1]], axis=2
    )
    in_shaped = grad_in_full.reshape((width,) + (2,) * level_list + (low_cols,))
    out_shaped = grad_out_full.reshape((2,) * level_list + (rank_size, 2 * hidden_part))
    in_axes = [level_list - step for step in range(level_list)]
    out_axes = [level_list - 1 - step for step in range(level_list)]
    grad_in, grad_out = reduce_parts(in_shaped, out_shaped, in_axes, out_axes, bit_order)
    grad_in = grad_in.reshape(width, low_cols)
    grad_out = grad_out.reshape(rank_size, 2 * hidden_part)
    returned = lax.all_to_all(
        out_rows.reshape(seq_count, slot_part, width).astype(jnp.bfloat16),
        "seq",
        split_axis=0,
        concat_axis=0,
        tiled=True,
    ).astype(jnp.float32)
    expert_rows = returned.reshape(experts_here, CAP, width)
    combined = jnp.einsum("xct,xcd->td", scaled_sel, expert_rows, precision=lax.Precision.HIGHEST)
    mixed = lax.psum_scatter(combined.astype(jnp.bfloat16), "ep", scatter_dimension=1, tiled=True)
    return (context, mixed, grad_in[None, None], grad_out[None, None])


def solution(mesh):
    return jax.shard_map(
        local,
        mesh=mesh,
        in_specs=(
            P("seq", "ep"),
            P("seq", "ep"),
            P("seq", "ep"),
            P("seq", None),
            P("seq", None),
            P("seq", None),
            P("seq", None),
            P("ep", "seq", None, None),
            P("ep", "seq", None, None),
            P("ep", "seq", None, None),
            P("ep", "seq", None, None),
        ),
        out_specs=(
            P("seq", "ep"),
            P("seq", "ep"),
            P("ep", "seq", None, None),
            P("ep", "seq", None, None),
        ),
        check_vma=False,
    )
```

profile of v0, /device:TPU:70, one launch (start us, length us, event | category | flops | bytes accessed | tf_op | source)
XLA Modules:
  0.0 874.6 jit_solution(15014008740312240719)
XLA Ops:
  12.0 11.6 %all-to-all-start.2 = ((bf16[64,5,2048]{2,1,0:T(8,128)(2,1)}), bf16[64,5,2048]{2,1,0:T(8,128)(2,1)}, u32[]{:S(2)}, u32[]{:S(2)}) async-start(bf16[64,5,2048]{2,1,0:T(8,128)(2,1)} %reshape.368), calls=%async_computation.2 | async-start | bytes 4194304 | tf_op jit(solution)/shard_map/all_to_all | solution.py:181
  30.0 14.5 %broadcast_in_dim.88 = bf16[1,602112]{1,0:T(2,128)(2,1)} reshape(bf16[602112]{0:T(1024)(128)(2,1)S(1)} %constant_dynamic-update-slice_fusion.1) | data formatting | bytes 2408448 | tf_op jit(solution)/shard_map/broadcast_in_dim | solution.py:92
  64.4 7.8 pad_maximum_fusion.7
  75.1 8.6 all-to-all-start.4
  83.8 7.5 pad_maximum_fusion.6
  100.0 82.7 %all-to-all-done.4 = bf16[64,5,2048]{2,1,0:T(8,128)(2,1)} async-done(((bf16[64,5,2048]{2,1,0:T(8,128)(2,1)}), bf16[64,5,2048]{2,1,0:T(8,128)(2,1)}, u32[]{:S(2)}, u32[]{:S(2)}) %all-to-all-start.4) | async-done | bytes 1310752 | tf_op jit(solution)/shard_map/all_to_all | solution.py:182
  182.7 9.5 %all-to-all-start = ((bf16[64,16,128]{2,1,0:T(8,128)(2,1)}), bf16[64,16,128]{2,1,0:T(8,128)(2,1)S(1)}, u32[]{:S(2)}, u32[]{:S(2)}) async-start(bf16[64,16,128]{2,1,0:T(8,128)(2,1)} %bitcast.8), calls=%async_computation | async-start | bytes 524288 | tf_op jit(solution)/shard_map/all_to_all | solution.py:51
  195.9 10.5 %pad_maximum_fusion.3 = bf16[4,602112]{1,0:T(4,128)(2,1)} fusion(bf16[2,602112]{1,0:T(2,128)(2,1)} %collective-permute-done.4, bf16[1,602112]{1,0:T(2,128)(2,1)} %collective-permute-done.3, bf16[1,602112]{1,0:T(2,128)(2,1)} %broadcast_in_dim.88), kind=kLoop, calls=%fused_computation.42 | loop fusion | flops 14450688 | bytes 9633792 | tf_op jit(solution)/shard_map/concatenate | solution.py:95
  206.9 58.6 %collective-permute-done.1 = bf16[2,634880]{1,0:T(2,128)(2,1)} collective-permute-done((bf16[2,634880]{1,0:T(2,128)(2,1)}, bf16[2,634880]{1,0:T(2,128)(2,1)}, u32[]{:S(2)}, u32[]{:S(2)}) %collective-permute-start.1) | collective-permute-done | bytes 2539552 | tf_op jit(solution)/shard_map/ppermute | solution.py:21
  265.5 10.8 %pad_maximum_fusion.2 = bf16[4,634880]{1,0:T(4,128)(2,1)} fusion(bf16[2,634880]{1,0:T(2,128)(2,1)} %collective-permute-done.1, bf16[1,634880]{1,0:T(2,128)(2,1)} %collective-permute-done, bf16[1,634880]{1,0:T(2,128)(2,1)S(1)} %broadcast_in_dim.83), kind=kLoop, calls=%fused_computation.41 | loop fusion | flops 15237120 | bytes 10158080 | tf_op jit(solution)/shard_map/concatenate | solution.py:95
  280.4 57.6 %while.15 = (s32[]{:T(128)}, f32[1,1024]{1,0:T(1,128)S(1)}, f32[1,1024]{1,0:T(1,128)S(1)}, f32[1,1024,128]{2,1,0:T(8,128)}, s32[8]{0:T(128)S(1)}, /*index=5*/bf1...) while((s32[]{:T(128)}, f32[1,1024]{1,0:T(1,128)S(1)}, ...), condition=%wide.region_3.4_spmd.clone, body=%wide.region_0.3_spmd.clone.sunk | while | flops 550918144 | bytes 18710740 | solution.py:80
  337.9 188.5 %collective-permute-done.5 = bf16[4,602112]{1,0:T(4,128)(2,1)} collective-permute-done((bf16[4,602112]{1,0:T(4,128)(2,1)}, bf16[4,602112]{1,0:T(4,128)(2,1)}, u32[]{:S(2)}, u32[]{:S(2)}) %collective-permute-start.5) | collective-permute-done | bytes 4816928 | tf_op jit(solution)/shard_map/ppermute | solution.py:21
  526.4 12.6 %pad_maximum_fusion.1 = bf16[8,602112]{1,0:T(8,128)(2,1)S(1)} fusion(bf16[4,602112]{1,0:T(4,128)(2,1)} %collective-permute-done.5, bf16[2,602112]{1,0:T(2,128)(2,1)} %collective-permute-done.4, bf16[1,602112]{1,0:T(2,128)(2,1)} %collective-permute-done.3, bf16[1,602112]{1,0:T(2,128)(2,1)} %broadcast_in_dim.88), kind=kLoop, calls=%fused_computation.40 | loop fusion | flops 38535168 | bytes 19267584 | tf_op jit(solution)/shard_map/concatenate | solution.py:95
  542.0 7.4 pad_maximum_fusion.4
  555.9 7.4 reshape.386
  563.3 6.6 copy.129
  574.9 7.5 reshape.388
  582.4 6.2 copy.130
  596.8 37.7 %collective-permute-done.2 = bf16[4,634880]{1,0:T(4,128)(2,1)} collective-permute-done((bf16[4,634880]{1,0:T(4,128)(2,1)}, bf16[4,634880]{1,0:T(4,128)(2,1)}, u32[]{:S(2)}, u32[]{:S(2)}) %collective-permute-start.2) | collective-permute-done | bytes 5079072 | tf_op jit(solution)/shard_map/ppermute | solution.py:21
  651.5 5.6 fusion.41
  663.8 13.0 %pad_maximum_fusion = bf16[8,634880]{1,0:T(8,128)(2,1)S(1)} fusion(bf16[4,634880]{1,0:T(4,128)(2,1)} %collective-permute-done.2, bf16[2,634880]{1,0:T(2,128)(2,1)} %collective-permute-done.1, bf16[1,634880]{1,0:T(2,128)(2,1)} %collective-permute-done, bf16[1,634880]{1,0:T(2,128)(2,1)S(1)} %broadcast_in_dim.83), kind=kLoop, calls=%fused_computation.39 | loop fusion | flops 40632320 | bytes 20316160 | tf_op jit(solution)/shard_map/concatenate | solution.py:95
  685.0 7.4 reshape.375
  692.4 6.2 copy.126
  708.8 7.4 reshape.378
  716.2 6.2 copy.128
  728.2 7.0 pad_maximum_fusion.5
  748.7 7.5 fusion.51
  757.8 13.8 %all-to-all-start.3 = ((bf16[64,5,2048]{2,1,0:T(8,128)(2,1)}), bf16[64,5,2048]{2,1,0:T(8,128)(2,1)}, u32[]{:S(2)}, u32[]{:S(2)}) async-start(bf16[64,5,2048]{2,1,0:T(8,128)(2,1)} %convert_element_type.77), calls=%async_computation.3 | async-start | bytes 4194304 | tf_op jit(solution)/shard_map/all_to_all | solution.py:277
  771.8 6.8 slice.188
  791.9 31.5 %collective-permute-done.7 = bf16[114688]{0:T(1024)(128)(2,1)S(1)} collective-permute-done((bf16[114688]{0:T(1024)(128)(2,1)S(1)}, bf16[114688]{0:T(1024)(128)(2,1)S(1)}, u32[]{:S(2)}, u32[]{:S(2)}) %collective-permute-start.7) | collective-permute-done | bytes 229408 | tf_op jit(solution)/shard_map/ppermute | solution.py:21
  827.9 9.4 %all-to-all-start.1 = ((bf16[64,2,1024]{2,1,0:T(2,128)(2,1)}), bf16[64,2,1024]{2,1,0:T(2,128)(2,1)S(1)}, u32[]{:S(2)}, u32[]{:S(2)}) async-start(bf16[64,2,1024]{2,1,0:T(2,128)(2,1)} %reshape.463), calls=%async_computation.1 | async-start | bytes 524288 | tf_op jit(solution)/shard_map/all_to_all | solution.py:83
  850.6 16.4 %reduce-scatter.2.cloned.1.call-done = bf16[128,512]{1,0:T(8,128)(2,1)} async-done(((bf16[128,2048]{1,0:T(8,128)(2,1)}), bf16[128,512]{1,0:T(8,128)(2,1)}) %reduce-scatter.2.cloned.1.call-update) | async-done | bytes 131088 | tf_op jit(solution)/shard_map/reduce_scatter | solution.py:286
  (362 shorter events, 222.5 us)
Async XLA Ops:
  8.0 272.4 %all-gather.3.cloned.1.call-start = ((), (), s32[]{:S(2)}) async-start(), calls=%async_computation.6 | async-start | bytes 2129920 | tf_op jit(solution)/shard_map/all_gather | solution.py:67
  9.9 47.8 %copy-start.27 = (s32[8,128]{1,0:T(8,128)}, s32[8,128]{1,0:T(8,128)S(1)}, u32[]{:S(2)}) copy-start(s32[8,128]{1,0:T(8,128)S(1)} %copy.124) | copy-start | bytes 12292
  12.0 11.7 %copy-start.26 = (bf16[1,1,64,384]{3,2,1,0:T(8,128)(2,1)S(1)}, bf16[1,1,64,384]{3,2,1,0:T(8,128)(2,1)}, u32[]{:S(2)}) copy-start(bf16[1,1,64,384]{3,2,1,0:T(8,128)(2,1)} %param.25) | copy-start | bytes 147460
  12.0 13.2 %copy-start.19 = (bf16[1,1,192,2048]{3,2,1,0:T(8,128)(2,1)S(1)}, bf16[1,1,192,2048]{3,2,1,0:T(8,128)(2,1)}, u32[]{:S(2)}) copy-start(bf16[1,1,192,2048]{3,2,1,0:T(8,128)(2,1)} %param.23) | copy-start | bytes 2359300
  12.0 14.0 %copy-start.6 = (bf16[1,1,2048,384]{3,2,1,0:T(8,128)(2,1)S(1)}, bf16[1,1,2048,384]{3,2,1,0:T(8,128)(2,1)}, u32[]{:S(2)}) copy-start(bf16[1,1,2048,384]{3,2,1,0:T(8,128)(2,1)} %param.22) | copy-start | bytes 4718596
  12.0 63.1 %all-to-all-start.2 = ((bf16[64,5,2048]{2,1,0:T(8,128)(2,1)}), bf16[64,5,2048]{2,1,0:T(8,128)(2,1)}, u32[]{:S(2)}, u32[]{:S(2)}) async-start(bf16[64,5,2048]{2,1,0:T(8,128)(2,1)} %reshape.368), calls=%async_computation.2 | async-start | bytes 4194304 | tf_op jit(solution)/shard_map/all_to_all | solution.py:181
  23.7 256.7 %all-gather.5.cloned.1.call-start = ((), (), s32[]{:S(2)}) async-start(), calls=%async_computation.7 | async-start | bytes 2129920 | tf_op jit(solution)/shard_map/all_gather | solution.py:68
  44.6 19.9 %collective-permute-start.3 = (bf16[1,602112]{1,0:T(2,128)(2,1)}, bf16[1,602112]{1,0:T(2,128)(2,1)}, u32[]{:S(2)}, u32[]{:S(2)}) collective-permute-start(bf16[1,602112]{1,0:T(2,128)(2,1)} %broadcast_in_dim.88), channel_id=1, source_target_pairs={{0,4},{4,0},{8,12},{12,8},{16,20},{20,16},{24,28},{28,24},{32,36},... | collective-permute-start | bytes 3612680 | tf_op jit(solution)/shard_map/ppermute | solution.py:21
  48.7 8.1 copy-start.25
  51.3 6.3 copy-start.41
  51.3 6.4 copy-start.36
  55.0 28.8 %collective-permute-start = (bf16[1,634880]{1,0:T(2,128)(2,1)S(1)}, bf16[1,634880]{1,0:T(2,128)(2,1)}, u32[]{:S(2)}, u32[]{:S(2)}) collective-permute-start(bf16[1,634880]{1,0:T(2,128)(2,1)S(1)} %broadcast_in_dim.83), channel_id=1, source_target_pairs={{0,4},{4,0},{8,12},{12,8},{16,20},{20,16},{24,28},{28,24},{32,36},... | collective-permute-start | bytes 3809288 | tf_op jit(solution)/shard_map/ppermute | solution.py:21
  57.7 6.7 copy-start.33
  72.3 123.7 %collective-permute-start.4 = (bf16[2,602112]{1,0:T(2,128)(2,1)}, bf16[2,602112]{1,0:T(2,128)(2,1)}, u32[]{:S(2)}, u32[]{:S(2)}) collective-permute-start(bf16[2,602112]{1,0:T(2,128)(2,1)} %pad_maximum_fusion.7), channel_id=1, source_target_pairs={{0,8},{8,0},{4,12},{12,4},{16,24},{24,16},{20,28},{28,20},{32,40},... | collective-permute-start | bytes 7225352 | tf_op jit(solution)/shard_map/ppermute | solution.py:21
  75.1 107.6 %all-to-all-start.4 = ((bf16[64,5,2048]{2,1,0:T(8,128)(2,1)}), bf16[64,5,2048]{2,1,0:T(8,128)(2,1)}, u32[]{:S(2)}, u32[]{:S(2)}) async-start(bf16[64,5,2048]{2,1,0:T(8,128)(2,1)} %reshape.392), calls=%async_computation.5 | async-start | bytes 4194304 | tf_op jit(solution)/shard_map/all_to_all | solution.py:182
  91.3 174.3 %collective-permute-start.1 = (bf16[2,634880]{1,0:T(2,128)(2,1)}, bf16[2,634880]{1,0:T(2,128)(2,1)}, u32[]{:S(2)}, u32[]{:S(2)}) collective-permute-start(bf16[2,634880]{1,0:T(2,128)(2,1)} %pad_maximum_fusion.6), channel_id=1, source_target_pairs={{0,8},{8,0},{4,12},{12,4},{16,24},{24,16},{20,28},{28,20},{32,40},... | collective-permute-start | bytes 7618568 | tf_op jit(solution)/shard_map/ppermute | solution.py:21
  182.7 97.6 %all-to-all-start = ((bf16[64,16,128]{2,1,0:T(8,128)(2,1)}), bf16[64,16,128]{2,1,0:T(8,128)(2,1)S(1)}, u32[]{:S(2)}, u32[]{:S(2)}) async-start(bf16[64,16,128]{2,1,0:T(8,128)(2,1)} %bitcast.8), calls=%async_computation | async-start | bytes 524288 | tf_op jit(solution)/shard_map/all_to_all | solution.py:51
  206.4 320.1 %collective-permute-start.5 = (bf16[4,602112]{1,0:T(4,128)(2,1)}, bf16[4,602112]{1,0:T(4,128)(2,1)}, u32[]{:S(2)}, u32[]{:S(2)}) collective-permute-start(bf16[4,602112]{1,0:T(4,128)(2,1)} %pad_maximum_fusion.3), channel_id=1, source_target_pairs={{0,16},{16,0},{4,20},{20,4},{8,24},{24,8},{12,28},{28,12},{32,48},... | collective-permute-start | bytes 14450696 | tf_op jit(solution)/shard_map/ppermute | solution.py:21
  276.3 358.2 %collective-permute-start.2 = (bf16[4,634880]{1,0:T(4,128)(2,1)}, bf16[4,634880]{1,0:T(4,128)(2,1)}, u32[]{:S(2)}, u32[]{:S(2)}) collective-permute-start(bf16[4,634880]{1,0:T(4,128)(2,1)} %pad_maximum_fusion.2), channel_id=1, source_target_pairs={{0,16},{16,0},{4,20},{20,4},{8,24},{24,8},{12,28},{28,12},{32,48},... | collective-permute-start | bytes 15237128 | tf_op jit(solution)/shard_map/ppermute | solution.py:21
  726.9 8.3 copy-start.13
  728.1 7.1 copy-start.14
  728.2 7.1 copy-start.12
  748.7 22.9 %collective-permute-start.6 = (bf16[229376]{0:T(1024)(128)(2,1)}, bf16[229376]{0:T(1024)(128)(2,1)S(1)}, u32[]{:S(2)}, u32[]{:S(2)}) collective-permute-start(bf16[229376]{0:T(1024)(128)(2,1)} %pad_maximum_fusion.10), channel_id=1, source_target_pairs={{0,4},{4,0},{8,12},{12,8},{16,20},{20,16},{24,28},{28,24},{32,36},... | collective-permute-start | bytes 1376264 | tf_op jit(solution)/shard_map/ppermute | solution.py:21
  757.8 70.1 %all-to-all-start.3 = ((bf16[64,5,2048]{2,1,0:T(8,128)(2,1)}), bf16[64,5,2048]{2,1,0:T(8,128)(2,1)}, u32[]{:S(2)}, u32[]{:S(2)}) async-start(bf16[64,5,2048]{2,1,0:T(8,128)(2,1)} %convert_element_type.77), calls=%async_computation.3 | async-start | bytes 4194304 | tf_op jit(solution)/shard_map/all_to_all | solution.py:277
  786.2 37.2 %collective-permute-start.7 = (bf16[114688]{0:T(1024)(128)(2,1)S(1)}, bf16[114688]{0:T(1024)(128)(2,1)S(1)}, u32[]{:S(2)}, u32[]{:S(2)}) collective-permute-start(bf16[114688]{0:T(1024)(128)(2,1)S(1)} %pad_maximum_fusion.11), channel_id=1, source_target_pairs={{0,8},{8,0},{4,12},{12,4},{16,24},{24,16},{20,28},{28,20},{32,40},... | collective-permute-start | bytes 688136 | tf_op jit(solution)/shard_map/ppermute | solution.py:21
  827.2 12.7 %copy-start.28 = (s32[8,128]{1,0:T(8,128)S(1)}, s32[8,128]{1,0:T(8,128)}, u32[]{:S(2)}) copy-start(s32[8,128]{1,0:T(8,128)} %copy-done.27) | copy-start | bytes 12292
  827.2 12.7 %copy-start.34 = (f32[128,8]{0,1:T(8,128)S(1)}, f32[128,8]{0,1:T(8,128)}, u32[]{:S(2)}) copy-start(f32[128,8]{0,1:T(8,128)} %copy-done.33) | copy-start | bytes 12292
  827.2 12.7 %copy-start.37 = (pred[8,128]{1,0:T(8,128)(4,1)S(1)}, pred[8,128]{1,0:T(8,128)(4,1)}, u32[]{:S(2)}) copy-start(pred[8,128]{1,0:T(8,128)(4,1)} %copy-done.35) | copy-start | bytes 3076
  827.9 19.3 %all-to-all-start.1 = ((bf16[64,2,1024]{2,1,0:T(2,128)(2,1)}), bf16[64,2,1024]{2,1,0:T(2,128)(2,1)S(1)}, u32[]{:S(2)}, u32[]{:S(2)}) async-start(bf16[64,2,1024]{2,1,0:T(2,128)(2,1)} %reshape.463), calls=%async_computation.1 | async-start | bytes 524288 | tf_op jit(solution)/shard_map/all_to_all | solution.py:83
  837.3 29.7 %reduce-scatter.2.cloned.1.call-start = ((), (), s32[]{:S(2)}) async-start(), calls=%async_computation.8 | async-start | bytes 655360 | tf_op jit(solution)/shard_map/reduce_scatter | solution.py:286
  841.9 6.7 collective-permute-start.8
  847.4 19.6 %copy-start.1 = (bf16[128,2048]{1,0:T(8,128)(2,1)S(1)}, bf16[128,2048]{1,0:T(8,128)(2,1)}, u32[]{:S(2)}) copy-start(bf16[128,2048]{1,0:T(8,128)(2,1)} %param.18) | copy-start | bytes 1572868
  (41 other events, 93.3 us)
Sparse Core Ops, SparseCore 0:
  11.6 82.0 all-gather.2
  96.5 77.7 all-gather.4
Sparse Core Ops, SparseCore 1:
  841.9 25.0 reduce-scatter.1
where the time goes:
time: 887 us; the launch traced here: 875 us
  waiting for transfers between devices  423 us (48%)
  local copies, waits for them, and re-layouts  188 us (21%)
  other arithmetic  101 us (11%)
  matrix products  82.5 us (9%)
  starting transfers between devices  63.7 us (7%)
  between operations  16.9 us (2%)
    ppermute x9, waiting for transfers between devices, from_partner(): return lax.ppermute(block, axis, route)  317 us
    all_to_all x1, waiting for transfers between devices, local(): lax.all_to_all(send_grads, 'seq', split_axis=0, concat_axis=0, tiled=True)  82.7 us
    reshape x14, local copies, waits for them, and re-layouts, unpack_parts(): stack[:, offset:offset + count].reshape((stack.shape[0],) + tuple(shape))  65.8 us
    concatenate x6, other arithmetic, collect_parts(): stack = jnp.concatenate([stack, other], axis=0)  62.2 us
    unnamed x103, local copies, waits for them, and re-layouts  30.2 us
    unnamed x5, matrix products  19.4 us
    dot_general x8, matrix products, absorb_block(): jnp.einsum('uqn,nd->uqd', weights.astype(jnp.bfloat16), value_block, pref...  18.6 us
    slice x5, other arithmetic, unpack_parts(): stack[:, offset:offset + count].reshape((stack.shape[0],) + tuple(shape))  18.3 us
  transfers between devices with their start and end apart: 17, of which 9 were waited for; matrix products, arithmetic and copies ran while one was open for 29% of the time, Pallas kernels for 0%

commit v1 on v0

v1 whole, which is shorter than its diff:
```python
import jax
import jax.numpy as jnp
from jax import lax
from jax.experimental import pallas as pl
from jax.experimental.pallas import tpu as pltpu
from jax.sharding import PartitionSpec as P

BF = jnp.bfloat16
F32 = jnp.float32
MESH = pl.DeviceIdType.MESH

TOK = 128
D = 2048
HD = 128
HEADS = 8
FF = 192
BLK = 80
MAIN = 32
ROWS = 160
NX, NZ = 4, 8
PARTS = 8
LOWR = 16
RANK = 64
KEYS = 512
PIECES = 5


def dot(a, b, ca, cb):
    return lax.dot_general(a, b, (((ca,), (cb,)), ((), ())), preferred_element_type=F32)


def attention_kernel(q_ref, kv_ref, out_ref, top_ref, sum_ref, acc_ref):
    s = lax.axis_index("seq")
    scale = HD**-0.5 * 1.4426950408889634
    top_ref[...] = jnp.full_like(top_ref, -1e30)
    sum_ref[...] = jnp.zeros_like(sum_ref)
    acc_ref[...] = jnp.zeros_like(acc_ref)

    def absorb(block, masked):
        rows = pl.ds(pl.multiple_of(block * KEYS, KEYS), KEYS)
        keys = kv_ref[rows, :HD]
        vals = kv_ref[rows, HD:]
        if masked:
            kpos = block * KEYS + lax.broadcasted_iota(jnp.int32, (TOK, KEYS), 1)
            qpos = s * TOK + lax.broadcasted_iota(jnp.int32, (TOK, KEYS), 0)
            allowed = kpos <= qpos
        for h in range(HEADS):
            sc = dot(q_ref[:, h * HD : (h + 1) * HD], keys, 1, 1)
            if masked:
                sc = jnp.where(allowed, sc, -1e30)
            old = top_ref[h]
            new = jnp.maximum(old, jnp.max(sc, axis=1, keepdims=True))
            factor = jnp.exp2((old - new) * scale)
            w = jnp.exp2((sc - new[:, :1]) * scale)
            part = w[:, :HD]
            for j in range(1, KEYS // HD):
                part = part + w[:, j * HD : (j + 1) * HD]
            sum_ref[h] = sum_ref[h] * factor + part
            acc_ref[h] = acc_ref[h] * factor + dot(w.astype(BF), vals, 1, 0)
            top_ref[h] = new

    full = s // (KEYS // TOK)

    @pl.loop(0, full)
    def _(block):
        absorb(block, False)

    absorb(full, True)
    for h in range(HEADS):
        total = jnp.sum(sum_ref[h], axis=1, keepdims=True)
        out_ref[:, h * HD : (h + 1) * HD] = (acc_ref[h] / total).astype(BF)


def attend(queries, kv):
    vm = pl.BlockSpec(memory_space=pltpu.VMEM)
    return pl.pallas_call(
        attention_kernel,
        out_shape=jax.ShapeDtypeStruct((TOK, HEADS * HD), BF),
        in_specs=[vm, vm],
        out_specs=vm,
        scratch_shapes=[pltpu.VMEM((HEADS, TOK, HD), F32)] * 3,
        compiler_params=pltpu.CompilerParams(vmem_limit_bytes=32 << 20),
        cost_estimate=pl.CostEstimate(
            flops=4 * TOK * HEADS * HD * 8192, bytes_accessed=5 << 20, transcendentals=8 << 20
        ),
        name="attention",
    )(queries, kv)


def expert_kernel(
    hid, cot, routes, rw, wgu, wd, ain, aout,
    mixed_o, gin_o, gout_o,
    WG, WD, WA, WB, WBB, PL_, PR_, CF, CFT, SL,
    sendb, rowsb, X, C, acc, low, glow, gin, gout,
    retb, outb, gins, gouts, ginr, goutr, accm, mixs, mixr,
    ws, wr, lw, rs, rr, os_, orr, gs, gr, ys, yr,
):
    s = lax.axis_index("seq")
    e = lax.axis_index("ep")
    x = s // 16
    z = lax.rem(s // 2, 8)
    c = lax.rem(s, 2)
    zh = z // 4
    lz = lax.rem(z, 4)
    site = jnp.logical_or(lz == 1, lz == 2)
    site_i = site.astype(jnp.int32)
    side = jnp.where(lz >= 2, 1, 0)
    step = jnp.where(lz >= 2, 1, -1)
    my_expert = x * 2 + zh

    def dev(xx, zz, cc):
        return ((xx * NZ + zz) * 2 + cc, e)

    def in_group(l, cc):
        return dev(x, zh * 4 + l, cc)

    q = lax.rem((z + 2) // 4, 2)

    def site_of(n):
        xx = n // 2
        zz2 = lax.rem(n, 2)
        l = jnp.where(zz2 == 0, 1 + q, 2 - q)
        zs = zz2 * 4 + l
        way = jnp.where(l == 1, -1, 1)
        i = lax.rem((z - zs) * way + 8, 8)
        return xx, zs, i

    def source_of(i, xx):
        zz = lax.rem(z + step * i + 8, 8)
        return xx, zz

    barrier = pltpu.get_barrier_semaphore()

    def greet(device):
        pl.semaphore_signal(barrier, inc=1, device_id=device, device_id_type=MESH)

    for d in range(1, 8):
        k = lax.rem(lz * 2 + c + d, 8)
        greet(in_group(k // 2, lax.rem(k, 2)))
    for d in range(1, 4):
        greet((s, lax.rem(e + d, 4)))

    @pl.loop(0, 8)
    def _(n):
        xx, zs, _i = site_of(n)

        @pl.when(jnp.logical_not(jnp.logical_and(site, n == my_expert)))
        def _():
            greet(dev(xx, zs, c))

    @pl.when(site)
    def _():
        @pl.loop(0, 16)
        def _(j):
            xx, zz = source_of(j // 4, lax.rem(j, 4))

            @pl.when(jnp.logical_not(jnp.logical_and(j // 4 == 0, xx == x)))
            def _():
                greet(dev(xx, zz, c))

    pl.semaphore_wait(barrier, 18 + 14 * site_i)

    def slot(k, p):
        if p == 0:
            return WG.at[k, pl.ds(0, D // 2)]
        if p == 1:
            return WG.at[k, pl.ds(D // 2, D // 2)]
        return (WD, WA, WB)[p - 2].at[k]

    def own(p):
        if p == 0:
            return wgu.at[pl.ds(0, D // 2)]
        if p == 1:
            return wgu.at[pl.ds(D // 2, D // 2)]
        return (wd, ain, aout)[p - 2]

    def wcopy(src, k, p, role, device):
        return pltpu.make_async_remote_copy(
            src_ref=src, dst_ref=slot(k, p), send_sem=ws.at[role, p], recv_sem=wr.at[k, p],
            device_id=device, device_id_type=MESH,
        )

    sibling = in_group(lz, 1 - c)
    inner = in_group(3 - lz, c)
    feed = in_group(1 + jnp.where(site, 1 - side, side), c)
    mine = lz * 2 + c
    outer_l = side * 3
    k_outer = outer_l * 2 + c
    k_inner = (3 - lz) * 2 + c
    k_far = (3 - outer_l) * 2 + c
    order = (2, 0, 1, 3, 4)

    for p in order:
        wcopy(own(p), mine, p, 0, feed).start()

    def local_w(p):
        return pltpu.make_async_copy(own(p), slot(mine, p), lw.at[p])

    @pl.when(site)
    def _():
        for p in order:
            wcopy(own(p), mine, p, 1, sibling).start()
        for p in order:
            local_w(p).start()

    lane = lax.broadcasted_iota(jnp.int32, (TOK, TOK), 1)
    sub = lax.broadcasted_iota(jnp.int32, (TOK, TOK), 0)
    ids = lane + e * 8
    chosen = jnp.zeros((TOK, TOK), F32)
    coef = jnp.zeros((TOK, TOK), F32)
    for j in range(8):
        hit = routes[:, j : j + 1] == ids
        chosen = chosen + jnp.where(hit, 1.0, 0.0)
        coef = coef + jnp.where(hit, rw[:, j : j + 1], 0.0)
    chosen_t = chosen.T
    before = jnp.where(sub < lane, 1.0, 0.0).astype(BF)
    slot_t = dot(chosen_t.astype(BF), before, 1, 0)
    SL[...] = jnp.where(chosen_t > 0.5, slot_t, 1000.0)
    CF[...] = coef
    CFT[...] = coef.T

    row = lax.broadcasted_iota(jnp.int32, (BLK, TOK), 0)
    tail = row >= 2 * MAIN
    first = jnp.where(tail, row - MAIN, row)
    is_l = jnp.logical_or(row < MAIN, jnp.logical_and(tail, row < 2 * MAIN + 8))
    is_r = jnp.logical_not(is_l)
    target_l = jnp.where(is_l, first, -1).astype(F32)
    target_r = jnp.where(is_r, jnp.where(tail, row - MAIN - 8, row - MAIN), -1).astype(F32)

    def row_copy(n, xx, zs, i):
        return pltpu.make_async_remote_copy(
            src_ref=sendb.at[n], dst_ref=rowsb.at[i, x], send_sem=rs.at[n], recv_sem=rr.at[i, x],
            device_id=dev(xx, zs, c), device_id_type=MESH,
        )

    def is_own(n):
        return jnp.logical_and(site, n == my_expert)

    @pl.loop(0, 8)
    def _(n):
        slots = SL[pl.ds(n, 1), :]
        p_l = jnp.where(slots == target_l, 1.0, 0.0)
        p_r = jnp.where(slots == target_r, 1.0, 0.0)
        coef_r = jnp.sum(p_r * CFT[pl.ds(n, 1), :], axis=1, keepdims=True)
        p_l = p_l.astype(BF)
        p_r = p_r.astype(BF)
        PL_[n] = p_l
        PR_[n] = p_r
        block = (dot(p_l, hid[...], 1, 0) + dot(p_r, cot[...], 1, 0) * coef_r).astype(BF)
        xx, zs, i = site_of(n)

        @pl.when(is_own(n))
        def _():
            rowsb[0, x] = block

        @pl.when(jnp.logical_not(is_own(n)))
        def _():
            sendb[n] = block
            row_copy(n, xx, zs, i).start()

    def arrived(k, p):
        wcopy(slot(k, p), k, p, 0, sibling).wait_recv()

    @pl.when(site)
    def _():
        for p in order:
            arrived(k_outer, p)
            wcopy(slot(k_outer, p), k_outer, p, 2, inner).start()
            wcopy(slot(k_outer, p), k_outer, p, 3, sibling).start()
        for p in order:
            arrived(k_inner, p)
            wcopy(slot(k_inner, p), k_inner, p, 4, sibling).start()
        for p in order:
            arrived(k_far, p)
            wcopy(slot(k_far, p), k_far, p, 5, sibling).start()
        for p in order:
            local_w(p).wait()

        @pl.loop(0, 4)
        def _(l):
            for p in order:
                arrived(l * 2 + 1 - c, p)

        lanes = lax.broadcasted_iota(jnp.int32, (RANK, 2 * FF), 1)
        gin[...] = jnp.zeros_like(gin)
        gout[...] = jnp.zeros_like(gout)

        @pl.loop(0, PARTS)
        def _(k):
            b = WB[k].astype(F32)
            WBB[k, pl.ds(0, RANK)] = jnp.where(lanes < FF, b, 0.0).astype(BF)
            WBB[k, pl.ds(RANK, RANK)] = jnp.where(lanes >= FF, b, 0.0).astype(BF)

        @pl.loop(0, 4)
        def _(i):
            @pl.loop(0, 4)
            def _(xx):
                @pl.when(jnp.logical_not(jnp.logical_and(i == 0, xx == x)))
                def _():
                    pltpu.make_async_remote_copy(
                        src_ref=rowsb.at[i, xx], dst_ref=rowsb.at[i, xx], send_sem=rs.at[0],
                        recv_sem=rr.at[i, xx], device_id=sibling, device_id_type=MESH,
                    ).wait_recv()

            for j in range(4):
                X[j * MAIN : (j + 1) * MAIN] = rowsb[i, j, 0:MAIN]
                C[j * MAIN : (j + 1) * MAIN] = rowsb[i, j, MAIN : 2 * MAIN]
            for j in range(2):
                t0 = rowsb[i, 2 * j, 2 * MAIN : BLK].astype(F32)
                t1 = rowsb[i, 2 * j + 1, 2 * MAIN : BLK].astype(F32)
                at = 4 * MAIN + 16 * j
                X[at : at + 16] = jnp.concatenate([t0[:8], t1[:8]], axis=0).astype(BF)
                C[at : at + 16] = jnp.concatenate([t0[8:], t1[8:]], axis=0).astype(BF)
            rows = X[...]
            low[...] = dot(rows, WA[...].reshape(PARTS * LOWR, D), 1, 1).astype(BF)
            glow[...] = jnp.zeros_like(glow)
            acc[...] = jnp.zeros_like(acc)

            @pl.loop(0, PARTS)
            def _(k):
                lo = low[...]
                pre = dot(X[...], WG[k], 1, 0) + dot(lo, WBB[k], 1, 0)
                g = pre[:, :FF]
                u = pre[:, FF:]
                back = dot(C[...], WD[k], 1, 1)
                sig = 1.0 / (1.0 + jnp.exp(-g))
                silu = g * sig
                acc[...] += dot((silu * u).astype(BF), WD[k], 1, 0)
                dg = back * u * sig * (1.0 + g * (1.0 - sig))
                du = back * silu
                dgu = jnp.concatenate([dg, du], axis=1).astype(BF)
                r = dot(lo, dgu, 0, 0)
                gout[k] += jnp.where(lanes < FF, r[:RANK], r[RANK:])
                glow[...] += dot(dgu, WBB[k], 1, 1)

            gin[...] += dot(glow[...].astype(BF), X[...], 0, 0)

            for j in range(4):
                xx, zz = source_of(i, j)
                a = acc[j * MAIN : (j + 1) * MAIN].astype(BF)
                t = acc[4 * MAIN + 8 * j : 4 * MAIN + 8 * j + 8]
                t = jnp.concatenate([t[:, : D // 2], t[:, D // 2 :]], axis=0).astype(BF)
                mine_too = jnp.logical_and(i == 0, x == j)

                @pl.when(mine_too)
                def _():
                    outb[my_expert, 0:MAIN] = a[:, : D // 2]
                    outb[my_expert, MAIN : 2 * MAIN] = a[:, D // 2 :]
                    outb[my_expert, 2 * MAIN : BLK] = t

                @pl.when(jnp.logical_not(mine_too))
                def _():
                    retb[i, j, 0:MAIN] = a[:, : D // 2]
                    retb[i, j, MAIN : 2 * MAIN] = a[:, D // 2 :]
                    retb[i, j, 2 * MAIN : BLK] = t
                    pltpu.make_async_remote_copy(
                        src_ref=retb.at[i, j], dst_ref=outb.at[my_expert], send_sem=os_.at[i, j],
                        recv_sem=orr.at[my_expert], device_id=dev(xx, zz, c), device_id_type=MESH,
                    ).start()

        here = side * 2 + c

        def grad_copies(k):
            device = in_group(k // 2, lax.rem(k, 2))
            return [
                pltpu.make_async_remote_copy(
                    src_ref=src.at[k], dst_ref=dst.at[here], send_sem=gs.at[k, p],
                    recv_sem=gr.at[here, p], device_id=device, device_id_type=MESH,
                )
                for p, (src, dst) in enumerate(((gins, ginr), (gouts, goutr)))
            ]

        gins[...] = gin[...].reshape(PARTS, LOWR, D).astype(BF)
        gouts[...] = gout[...].astype(BF)

        @pl.loop(0, PARTS)
        def _(k):
            @pl.when(k == mine)
            def _():
                ginr[here] = gins[k]
                goutr[here] = gouts[k]

            @pl.when(k != mine)
            def _():
                for copy in grad_copies(k):
                    copy.start()

    accm[...] = jnp.zeros_like(accm)

    @pl.loop(0, 8)
    def _(n):
        @pl.when(jnp.logical_not(is_own(n)))
        def _():
            pltpu.make_async_remote_copy(
                src_ref=outb.at[n], dst_ref=outb.at[n], send_sem=rs.at[0], recv_sem=orr.at[n],
                device_id=sibling, device_id_type=MESH,
            ).wait_recv()

        cf = jnp.sum(jnp.where(lane == n, CF[...], 0.0), axis=1, keepdims=True)
        block = outb[n]
        accm[:, : D // 2] += cf * dot(PL_[n], block, 0, 0)
        accm[:, D // 2 :] += cf * dot(PR_[n], block, 0, 0)

    def y_copy(d):
        to = lax.rem(e + d, 4)
        return pltpu.make_async_remote_copy(
            src_ref=mixs.at[to], dst_ref=mixr.at[d - 1], send_sem=ys.at[d - 1], recv_sem=yr.at[d - 1],
            device_id=(s, to), device_id_type=MESH,
        )

    for yy in range(4):
        mixs[yy] = accm[:, yy * 512 : (yy + 1) * 512].astype(BF)
    for d in (2, 1, 3):
        y_copy(d).start()

    for n in range(4):
        self_site = jnp.logical_and(site, n == side * 2 + c)

        @pl.when(jnp.logical_not(self_site))
        def _():
            for p, dst in enumerate((ginr, goutr)):
                pltpu.make_async_remote_copy(
                    src_ref=dst.at[n], dst_ref=dst.at[n], send_sem=rs.at[0], recv_sem=gr.at[n, p],
                    device_id=sibling, device_id_type=MESH,
                ).wait_recv()

    gin_o[...] = sum([ginr[n].astype(F32) for n in range(1, 4)], ginr[0].astype(F32))
    gout_o[...] = sum([goutr[n].astype(F32) for n in range(1, 4)], goutr[0].astype(F32))

    total = accm[:, pl.ds(pl.multiple_of(e * 512, 512), 512)]
    for d in range(1, 4):
        y_copy(d).wait_recv()
        total = total + mixr[d - 1].astype(F32)
    mixed_o[...] = total.astype(BF)

    for d in range(1, 4):
        y_copy(d).wait_send()
    for p in order:
        wcopy(own(p), mine, p, 0, feed).wait_send()

    @pl.loop(0, 8)
    def _(n):
        xx, zs, i = site_of(n)

        @pl.when(jnp.logical_not(is_own(n)))
        def _():
            row_copy(n, xx, zs, i).wait_send()

    @pl.when(site)
    def _():
        for p in order:
            wcopy(own(p), mine, p, 1, sibling).wait_send()
            for role in range(2, 6):
                wcopy(slot(mine, p), mine, p, role, sibling).wait_send()

        @pl.loop(0, 4)
        def _(i):
            @pl.loop(0, 4)
            def _(j):
                @pl.when(jnp.logical_not(jnp.logical_and(i == 0, x == j)))
                def _():
                    pltpu.make_async_remote_copy(
                        src_ref=retb.at[i, j], dst_ref=outb.at[0], send_sem=os_.at[i, j],
                        recv_sem=orr.at[0], device_id=sibling, device_id_type=MESH,
                    ).wait_send()

        @pl.loop(0, PARTS)
        def _(k):
            @pl.when(k != mine)
            def _():
                for p, src in enumerate((gins, gouts)):
                    pltpu.make_async_remote_copy(
                        src_ref=src.at[k], dst_ref=src.at[k], send_sem=gs.at[k, p],
                        recv_sem=gr.at[0, p], device_id=sibling, device_id_type=MESH,
                    ).wait_send()


def experts(hidden, cotangent, routes, route_weight, wgu, wd, ain, aout):
    vm = pl.BlockSpec(memory_space=pltpu.VMEM)
    hbm = pl.BlockSpec(memory_space=pl.ANY)
    dma = pltpu.SemaphoreType.DMA
    v = pltpu.VMEM
    return pl.pallas_call(
        expert_kernel,
        out_shape=(
            jax.ShapeDtypeStruct((TOK, 512), BF),
            jax.ShapeDtypeStruct((LOWR, D), F32),
            jax.ShapeDtypeStruct((RANK, 2 * FF), F32),
        ),
        in_specs=[vm, vm, vm, vm, hbm, hbm, hbm, hbm],
        out_specs=(vm, vm, vm),
        scratch_shapes=[
            v((PARTS, D, 2 * FF), BF),
            v((PARTS, FF, D), BF),
            v((PARTS, LOWR, D), BF),
            v((PARTS, RANK, 2 * FF), BF),
            v((PARTS, 2 * RANK, 2 * FF), BF),
            v((8, BLK, TOK), BF),
            v((8, BLK, TOK), BF),
            v((TOK, TOK), F32),
            v((TOK, TOK), F32),
            v((TOK, TOK), F32),
            v((8, BLK, D), BF),
            v((4, NX, BLK, D), BF),
            v((ROWS, D), BF),
            v((ROWS, D), BF),
            v((ROWS, D), F32),
            v((ROWS, 2 * RANK), BF),
            v((ROWS, 2 * RANK), F32),
            v((PARTS * LOWR, D), F32),
            v((PARTS, RANK, 2 * FF), F32),
            v((4, NX, BLK, D // 2), BF),
            v((8, BLK, D // 2), BF),
            v((PARTS, LOWR, D), BF),
            v((PARTS, RANK, 2 * FF), BF),
            v((4, LOWR, D), BF),
            v((4, RANK, 2 * FF), BF),
            v((TOK, D), F32),
            v((4, TOK, 512), BF),
            v((3, TOK, 512), BF),
            dma((6, PIECES)),
            dma((PARTS, PIECES)),
            dma((PIECES,)),
            dma((8,)),
            dma((4, NX)),
            dma((4, NX)),
            dma((8,)),
            dma((PARTS, 2)),
            dma((4, 2)),
            dma((3,)),
            dma((3,)),
        ],
        compiler_params=pltpu.CompilerParams(
            collective_id=0, has_side_effects=True, vmem_limit_bytes=60 << 20
        ),
        cost_estimate=pl.CostEstimate(
            flops=16 << 30, bytes_accessed=32 << 20, transcendentals=1 << 20
        ),
        name="experts",
    )(hidden, cotangent, routes, route_weight, wgu, wd, ain, aout)


def local(
    queries, keys, values, hidden, cotangent, routes, route_weight,
    w_gate_up, w_down, adapter_in, adapter_out,
):
    kv = lax.all_gather(jnp.concatenate([keys, values], axis=1), "seq", axis=0, tiled=True)
    mixed, gin, gout = experts(
        hidden, cotangent, routes, route_weight,
        w_gate_up[0, 0], w_down[0, 0], adapter_in[0, 0].T, adapter_out[0, 0],
    )
    context = attend(queries, kv)
    return (context, mixed, gin.T[None, None], gout[None, None])


def solution(mesh):
    return jax.shard_map(
        local,
        mesh=mesh,
        in_specs=(
            P("seq", "ep"),
            P("seq", "ep"),
            P("seq", "ep"),
            P("seq", None),
            P("seq", None),
            P("seq", None),
            P("seq", None),
            P("ep", "seq", None, None),
            P("ep", "seq", None, None),
            P("ep", "seq", None, None),
            P("ep", "seq", None, None),
        ),
        out_specs=(
            P("seq", "ep"),
            P("seq", "ep"),
            P("ep", "seq", None, None),
            P("ep", "seq", None, None),
        ),
        check_vma=False,
    )
```

time: 887 us -> 309 us (0.35)
  waiting for transfers between devices: 423 us -> 0.04 us
  Pallas kernels: 0 us -> 282 us
  local copies, waits for them, and re-layouts: 188 us -> 6.98 us
  other arithmetic: 101 us -> 1.41 us
  matrix products: 82.5 us -> 0 us
  starting transfers between devices: 63.7 us -> 0.04 us
    ppermute x9 -> x0, waiting for transfers between devices: 317 us -> none  [from_partner(): return lax.ppermute(block, axis, route)]
    pallas_call x0 -> x2, Pallas kernels: none -> 282 us  [the longest x1 242 us: experts(): pl.pallas_call(expert_kernel, out_shape=(jax.ShapeDtypeStruct((TOK, 512),...]
    reshape x37 -> x0, local copies, waits for them, and re-layouts: 91.7 us -> none  [the longest x14 65.8 us: unpack_parts(): stack[:, offset:offset + count].reshape((stack.shape[0],) + tuple(shape))]
    all_to_all x5 -> x0, waiting for transfers between devices: 88.8 us -> none  [the longest x1 82.7 us: local(): lax.all_to_all(send_grads, 'seq', split_axis=0, concat_axis=0, tiled=True)]
    dot_general x36 -> x0, matrix products: 63.2 us -> none  [the longest x8 18.6 us: absorb_block(): jnp.einsum('uqn,nd->uqd', weights.astype(jnp.bfloat16), value_block, pref...]
    concatenate x11 -> x1, other arithmetic: 63.4 us -> 1.41 us  [local(): jnp.concatenate([keys, values], axis=1)]
    all_to_all x5 -> x0, starting transfers between devices: 53 us -> none  [the longest x1 13.8 us: local(): lax.all_to_all(out_rows.reshape(seq_count, slot_part, width).astype(jnp.b...]
    slice x25 -> x0, local copies, waits for them, and re-layouts: 30.1 us -> none  [the longest x9 16.2 us: reduce_parts(): first = keep_first + incoming[:first_count].reshape(keep_first.shape)]
  transfers between devices with their start and end apart: 17 -> 1, of which waited for: 9 -> 0; matrix products, arithmetic and copies ran while one was open for 29% -> 1% of each run, Pallas kernels for 0% -> 80%
where the time goes in v1:
time: 309 us; the launch traced here: 305 us
  Pallas kernels  282 us (91%)
  between operations  14.1 us (5%)
  local copies, waits for them, and re-layouts  6.98 us (2%)
    pallas_call x1, Pallas kernels, experts(): pl.pallas_call(expert_kernel, out_shape=(jax.ShapeDtypeStruct((TOK, 512),...  242 us
    pallas_call x1, Pallas kernels, attend(): pl.pallas_call(attention_kernel, out_shape=jax.ShapeDtypeStruct((TOK, HEA...  39.9 us
    unnamed x15, local copies, waits for them, and re-layouts  6.98 us
  transfers between devices with their start and end apart: 1, of which 0 were waited for; matrix products, arithmetic and copies ran while one was open for 1% of the time, Pallas kernels for 80%

profile of v1, /device:TPU:70, one launch (start us, length us, event | category | flops | bytes accessed | tf_op | source)
XLA Modules:
  0.0 304.7 jit_solution(15306227659176977373)
XLA Ops:
  7.2 0.0 all-gather.2.cloned.1.call-start
  7.2 1.4 pad_maximum_fusion
  8.6 0.0 all-gather.2.cloned.1.call-update
  8.6 1.4 copy.15.routes
  10.1 1.4 copy.16.rw
  11.5 0.0 copy-start.1
  11.5 242.3 %experts.1 = (bf16[128,512]{1,0:T(8,128)(2,1)}, f32[16,2048]{1,0:T(8,128)}, f32[64,384]{1,0:T(8,128)}) custom-call(bf16[128,2048]{1,0:T(8,128)(2,1)} %hid.1, bf16[128,2048]{1,0:T(8,128)(2,1)} %cot.1, s32[128,8]{1,0:T(8,128)} %copy.15.routes, f32[128,8]{1,0:T(8,128)} %copy.16.rw, bf16[2048,384]{1,0:T(8,128)(2,1)} %bitcast.12, bf16[192,2048]{1,0:T(8,128)(2,1)} %bitcast.13, ...), custom_call_target="tpu_custom_call" | custom-call | flops 17179869184 | bytes 33554432 | tf_op jit(solution)/shard_map/experts/pallas_call | solution.py:483
  253.7 0.0 all-gather.2.cloned.1.call-done.kv_ref
  253.8 0.0 copy-done.1
  253.8 0.0 copy-start
  253.8 2.2 copy-done
  256.0 0.0 copy-start.3
  256.0 0.0 copy-start.2
  256.0 0.0 copy-start.4
  256.0 39.9 %attention.1 = bf16[128,1024]{1,0:T(8,128)(2,1)} custom-call(bf16[128,1024]{1,0:T(8,128)(2,1)S(1)} %copy-done.1, bf16[8192,256]{1,0:T(8,128)(2,1)S(1)} %copy-done), custom_call_target="tpu_custom_call" | custom-call | flops 4294967296 | bytes 5242880 | tf_op jit(solution)/shard_map/attention/pallas_call | solution.py:76
  295.9 0.0 copy-done.3
  295.9 0.7 copy.20
  296.5 0.0 copy-done.2
  296.5 0.7 copy.21
  297.2 0.0 copy-done.4
  297.2 0.6 copy.22
Async XLA Ops:
  7.2 246.6 %all-gather.2.cloned.1.call-start = ((), (), s32[]{:S(2)}) async-start(), calls=%async_computation | async-start | bytes 4259840 | tf_op jit(solution)/shard_map/all_gather | solution.py:547
  11.5 242.3 %copy-start.1 = (bf16[128,1024]{1,0:T(8,128)(2,1)S(1)}, bf16[128,1024]{1,0:T(8,128)(2,1)}, u32[]{:S(2)}) copy-start(bf16[128,1024]{1,0:T(8,128)(2,1)} %q_ref.1) | copy-start | bytes 786436
  253.8 2.2 copy-start
  256.0 39.9 %copy-start.3 = (bf16[128,512]{1,0:T(8,128)(2,1)S(1)}, bf16[128,512]{1,0:T(8,128)(2,1)}, u32[]{:S(2)}) copy-start(bf16[128,512]{1,0:T(8,128)(2,1)} %get-tuple-element.15) | copy-start | bytes 393220
  256.0 40.6 %copy-start.2 = (f32[16,2048]{1,0:T(8,128)S(1)}, f32[16,2048]{1,0:T(8,128)}, u32[]{:S(2)}) copy-start(f32[16,2048]{1,0:T(8,128)} %get-tuple-element.8) | copy-start | bytes 393220
  256.0 41.2 %copy-start.4 = (f32[64,384]{1,0:T(8,128)S(1)}, f32[64,384]{1,0:T(8,128)}, u32[]{:S(2)}) copy-start(f32[64,384]{1,0:T(8,128)} %get-tuple-element.9) | copy-start | bytes 294916
Sparse Core Ops, SparseCore 0:
  11.4 131.1 all-gather.1

commit v2 on v1

--- a/solution.py
+++ b/solution.py
@@ -21,7 +21,8 @@
 PARTS = 8
 LOWR = 16
 RANK = 64
-KEYS = 512
+KEYS = 1024
+SCALE = HD**-0.5 * 1.4426950408889634
 PIECES = 5
 
 
@@ -29,71 +30,14 @@
     return lax.dot_general(a, b, (((ca,), (cb,)), ((), ())), preferred_element_type=F32)
 
 
-def attention_kernel(q_ref, kv_ref, out_ref, top_ref, sum_ref, acc_ref):
-    s = lax.axis_index("seq")
-    scale = HD**-0.5 * 1.4426950408889634
-    top_ref[...] = jnp.full_like(top_ref, -1e30)
-    sum_ref[...] = jnp.zeros_like(sum_ref)
-    acc_ref[...] = jnp.zeros_like(acc_ref)
-
-    def absorb(block, masked):
-        rows = pl.ds(pl.multiple_of(block * KEYS, KEYS), KEYS)
-        keys = kv_ref[rows, :HD]
-        vals = kv_ref[rows, HD:]
-        if masked:
-            kpos = block * KEYS + lax.broadcasted_iota(jnp.int32, (TOK, KEYS), 1)
-            qpos = s * TOK + lax.broadcasted_iota(jnp.int32, (TOK, KEYS), 0)
-            allowed = kpos <= qpos
-        for h in range(HEADS):
-            sc = dot(q_ref[:, h * HD : (h + 1) * HD], keys, 1, 1)
-            if masked:
-                sc = jnp.where(allowed, sc, -1e30)
-            old = top_ref[h]
-            new = jnp.maximum(old, jnp.max(sc, axis=1, keepdims=True))
-            factor = jnp.exp2((old - new) * scale)
-            w = jnp.exp2((sc - new[:, :1]) * scale)
-            part = w[:, :HD]
-            for j in range(1, KEYS // HD):
-                part = part + w[:, j * HD : (j + 1) * HD]
-            sum_ref[h] = sum_ref[h] * factor + part
-            acc_ref[h] = acc_ref[h] * factor + dot(w.astype(BF), vals, 1, 0)
-            top_ref[h] = new
-
-    full = s // (KEYS // TOK)
-
-    @pl.loop(0, full)
-    def _(block):
-        absorb(block, False)
-
-    absorb(full, True)
-    for h in range(HEADS):
-        total = jnp.sum(sum_ref[h], axis=1, keepdims=True)
-        out_ref[:, h * HD : (h + 1) * HD] = (acc_ref[h] / total).astype(BF)
-
-
-def attend(queries, kv):
-    vm = pl.BlockSpec(memory_space=pltpu.VMEM)
-    return pl.pallas_call(
-        attention_kernel,
-        out_shape=jax.ShapeDtypeStruct((TOK, HEADS * HD), BF),
-        in_specs=[vm, vm],
-        out_specs=vm,
-        scratch_shapes=[pltpu.VMEM((HEADS, TOK, HD), F32)] * 3,
-        compiler_params=pltpu.CompilerParams(vmem_limit_bytes=32 << 20),
-        cost_estimate=pl.CostEstimate(
-            flops=4 * TOK * HEADS * HD * 8192, bytes_accessed=5 << 20, transcendentals=8 << 20
-        ),
-        name="attention",
-    )(queries, kv)
-
-
-def expert_kernel(
-    hid, cot, routes, rw, wgu, wd, ain, aout,
-    mixed_o, gin_o, gout_o,
+def kernel(
+    queries, keys, values, hid, cot, routes, rw, wgu, wd, ain, aout,
+    ctx_o, mixed_o, gin_o, gout_o,
+    kvb, QT, top, den, num,
     WG, WD, WA, WB, WBB, PL_, PR_, CF, CFT, SL,
     sendb, rowsb, X, C, acc, low, glow, gin, gout,
     retb, outb, gins, gouts, ginr, goutr, accm, mixs, mixr,
-    ws, wr, lw, rs, rr, os_, orr, gs, gr, ys, yr,
+    ws, wr, lw, rs, rr, os_, orr, gs, gr, ys, yr, kzs, kzr, kxs, kxr, kcs, kcr,
 ):
     s = lax.axis_index("seq")
     e = lax.axis_index("ep")
@@ -129,6 +73,10 @@
         zz = lax.rem(z + step * i + 8, 8)
         return xx, zz
 
+    place = x * NZ + z
+    kvb[place, c, :, 0:HD] = keys[...]
+    kvb[place, c, :, HD:] = values[...]
+
     barrier = pltpu.get_barrier_semaphore()
 
     def greet(device):
@@ -139,6 +87,9 @@
         greet(in_group(k // 2, lax.rem(k, 2)))
     for d in range(1, 4):
         greet((s, lax.rem(e + d, 4)))
+        greet(dev(lax.rem(x + d, 4), z, c))
+    for d in range(1, 8):
+        greet(dev(x, lax.rem(z + d, 8), c))
 
     @pl.loop(0, 8)
     def _(n):
@@ -158,7 +109,31 @@
             def _():
                 greet(dev(xx, zz, c))
 
-    pl.semaphore_wait(barrier, 18 + 14 * site_i)
+    pl.semaphore_wait(barrier, 28 + 14 * site_i)
+
+    def z_copy(d):
+        block = kvb.at[place, c]
+        return pltpu.make_async_remote_copy(
+            src_ref=block, dst_ref=block, send_sem=kzs.at[d - 1], recv_sem=kzr.at[d - 1],
+            device_id=dev(x, lax.rem(z + d, 8), c), device_id_type=MESH,
+        )
+
+    def x_copy(d):
+        block = kvb.at[pl.ds(x * NZ, NZ), c]
+        return pltpu.make_async_remote_copy(
+            src_ref=block, dst_ref=block, send_sem=kxs.at[d - 1], recv_sem=kxr.at[d - 1],
+            device_id=dev(lax.rem(x + d, 4), z, c), device_id_type=MESH,
+        )
+
+    def core_copy(d):
+        block = kvb.at[pl.ds(lax.rem(x + 4 - d, 4) * NZ, NZ), c]
+        return pltpu.make_async_remote_copy(
+            src_ref=block, dst_ref=block, send_sem=kcs.at[d], recv_sem=kcr.at[d],
+            device_id=dev(x, z, 1 - c), device_id_type=MESH,
+        )
+
+    for d in (4, 3, 5, 2, 6, 1, 7):
+        z_copy(d).start()
 
     def slot(k, p):
         if p == 0:
@@ -205,19 +180,18 @@
 
     lane = lax.broadcasted_iota(jnp.int32, (TOK, TOK), 1)
     sub = lax.broadcasted_iota(jnp.int32, (TOK, TOK), 0)
-    ids = lane + e * 8
+    ids = sub + e * 8
     chosen = jnp.zeros((TOK, TOK), F32)
     coef = jnp.zeros((TOK, TOK), F32)
     for j in range(8):
-        hit = routes[:, j : j + 1] == ids
+        hit = routes[j : j + 1, :] == ids
         chosen = chosen + jnp.where(hit, 1.0, 0.0)
-        coef = coef + jnp.where(hit, rw[:, j : j + 1], 0.0)
-    chosen_t = chosen.T
+        coef = coef + jnp.where(hit, rw[j : j + 1, :], 0.0)
     before = jnp.where(sub < lane, 1.0, 0.0).astype(BF)
-    slot_t = dot(chosen_t.astype(BF), before, 1, 0)
-    SL[...] = jnp.where(chosen_t > 0.5, slot_t, 1000.0)
-    CF[...] = coef
-    CFT[...] = coef.T
+    slots_of = dot(chosen.astype(BF), before, 1, 0)
+    SL[...] = jnp.where(chosen > 0.5, slots_of, 1000.0)
+    CF[...] = coef.T
+    CFT[...] = coef
 
     row = lax.broadcasted_iota(jnp.int32, (BLK, TOK), 0)
     tail = row >= 2 * MAIN
@@ -256,23 +230,102 @@
         @pl.when(jnp.logical_not(is_own(n)))
         def _():
             sendb[n] = block
-            row_copy(n, xx, zs, i).start()
+
+            @pl.when(i == 0)
+            def _():
+                row_copy(n, xx, zs, i).start()
+
+    for d in range(1, 8):
+        z_copy(d).wait_recv()
+    for d in (2, 1, 3):
+        x_copy(d).start()
+    core_copy(0).start()
+    for h in range(HEADS):
+        QT[h] = queries[:, h * HD : (h + 1) * HD].astype(F32).T.astype(BF)
+    top[...] = jnp.full_like(top, -1e30)
+    den[...] = jnp.zeros_like(den)
+    num[...] = jnp.zeros_like(num)
+    for d in (1, 3, 2):
+        x_copy(d).wait_recv()
+        core_copy(d).start()
+    for d in range(4):
+        core_copy(d).wait_recv()
+
+    def absorb(block, masked):
+        kv = kvb[pl.ds(block * (KEYS // 256), KEYS // 256)]
+        ks = kv[..., :HD].reshape(KEYS, HD)
+        vs = kv[..., HD:].reshape(KEYS, HD)
+        if masked:
+            kpos = block * KEYS + lax.broadcasted_iota(jnp.int32, (KEYS, TOK), 0)
+            qpos = s * TOK + lax.broadcasted_iota(jnp.int32, (KEYS, TOK), 1)
+            allowed = kpos <= qpos
+        for h in range(HEADS):
+            sc = dot(ks, QT[h], 1, 0)
+            if masked:
+                sc = jnp.where(allowed, sc, -1e30)
+            old = top[h, 0:1]
+            new = jnp.maximum(old, jnp.max(sc, axis=0, keepdims=True))
+            factor = jnp.exp2((old - new) * SCALE)
+            w = jnp.exp2((sc - new) * SCALE)
+            den[h, 0:1] = den[h, 0:1] * factor + jnp.sum(w, axis=0, keepdims=True)
+            num[h] = num[h] * factor + dot(vs, w.astype(BF), 0, 0)
+            top[h, 0:1] = new
 
     def arrived(k, p):
         wcopy(slot(k, p), k, p, 0, sibling).wait_recv()
 
+    def from_outer(p):
+        arrived(k_outer, p)
+        wcopy(slot(k_outer, p), k_outer, p, 2, inner).start()
+        wcopy(slot(k_outer, p), k_outer, p, 3, sibling).start()
+
+    def from_inner(p):
+        arrived(k_inner, p)
+        wcopy(slot(k_inner, p), k_inner, p, 4, sibling).start()
+
+    def from_far(p):
+        arrived(k_far, p)
+        wcopy(slot(k_far, p), k_far, p, 5, sibling).start()
+
+    passing = [(f, ps) for f in (from_outer, from_inner, from_far) for ps in ((2,), (0,), (1, 3, 4))]
+    full = s // (KEYS // TOK)
+
+    @pl.loop(0, len(passing) - 1)
+    def _(t):
+        @pl.when(t < full)
+        def _():
+            absorb(t, False)
+
+        for j, (f, ps) in enumerate(passing[:-1]):
+
+            @pl.when(jnp.logical_and(site, t == j))
+            def _():
+                for p in ps:
+                    f(p)
+
+        @pl.when(t == 2)
+        def _():
+            @pl.when(jnp.logical_not(site))
+            def _():
+                for p in order:
+                    wcopy(own(p), mine, p, 0, feed).wait_send()
+
+            @pl.loop(0, 8)
+            def _(n):
+                xx, zs, i = site_of(n)
+
+                @pl.when(jnp.logical_and(jnp.logical_not(is_own(n)), i > 0))
+                def _():
+                    row_copy(n, xx, zs, i).start()
+
+    absorb(full, True)
+    for h in range(HEADS):
+        ctx_o[:, h * HD : (h + 1) * HD] = (num[h] / den[h, 0:1]).T.astype(BF)
+
     @pl.when(site)
     def _():
-        for p in order:
-            arrived(k_outer, p)
-            wcopy(slot(k_outer, p), k_outer, p, 2, inner).start()
-            wcopy(slot(k_outer, p), k_outer, p, 3, sibling).start()
-        for p in order:
-            arrived(k_inner, p)
-            wcopy(slot(k_inner, p), k_inner, p, 4, sibling).start()
-        for p in order:
-            arrived(k_far, p)
-            wcopy(slot(k_far, p), k_far, p, 5, sibling).start()
+        for p in passing[-1][1]:
+            from_far(p)
         for p in order:
             local_w(p).wait()
 
@@ -435,8 +488,12 @@
 
     for d in range(1, 4):
         y_copy(d).wait_send()
-    for p in order:
-        wcopy(own(p), mine, p, 0, feed).wait_send()
+    for d in range(1, 8):
+        z_copy(d).wait_send()
+    for d in range(1, 4):
+        x_copy(d).wait_send()
+    for d in range(4):
+        core_copy(d).wait_send()
 
     @pl.loop(0, 8)
     def _(n):
@@ -449,6 +506,7 @@
     @pl.when(site)
     def _():
         for p in order:
+            wcopy(own(p), mine, p, 0, feed).wait_send()
             wcopy(own(p), mine, p, 1, sibling).wait_send()
             for role in range(2, 6):
                 wcopy(slot(mine, p), mine, p, role, sibling).wait_send()
@@ -475,21 +533,27 @@
                     ).wait_send()
 
 
-def experts(hidden, cotangent, routes, route_weight, wgu, wd, ain, aout):
+def run(queries, keys, values, hidden, cotangent, routes, route_weight, wgu, wd, ain, aout):
     vm = pl.BlockSpec(memory_space=pltpu.VMEM)
     hbm = pl.BlockSpec(memory_space=pl.ANY)
     dma = pltpu.SemaphoreType.DMA
     v = pltpu.VMEM
     return pl.pallas_call(
-        expert_kernel,
+        kernel,
         out_shape=(
+            jax.ShapeDtypeStruct((TOK, HEADS * HD), BF),
             jax.ShapeDtypeStruct((TOK, 512), BF),
             jax.ShapeDtypeStruct((LOWR, D), F32),
             jax.ShapeDtypeStruct((RANK, 2 * FF), F32),
         ),
-        in_specs=[vm, vm, vm, vm, hbm, hbm, hbm, hbm],
-        out_specs=(vm, vm, vm),
+        in_specs=[vm] * 7 + [hbm] * 4,
+        out_specs=(vm,) * 4,
         scratch_shapes=[
+            v((NX * NZ, 2, TOK, 2 * HD), BF),
+            v((HEADS, HD, TOK), BF),
+            v((HEADS, 8, TOK), F32),
+            v((HEADS, 8, TOK), F32),
+            v((HEADS, HD, TOK), F32),
             v((PARTS, D, 2 * FF), BF),
             v((PARTS, FF, D), BF),
             v((PARTS, LOWR, D), BF),
@@ -529,6 +593,12 @@
             dma((4, 2)),
             dma((3,)),
             dma((3,)),
+            dma((7,)),
+            dma((7,)),
+            dma((3,)),
+            dma((3,)),
+            dma((4,)),
+            dma((4,)),
         ],
         compiler_params=pltpu.CompilerParams(
             collective_id=0, has_side_effects=True, vmem_limit_bytes=60 << 20
@@ -536,20 +606,18 @@
         cost_estimate=pl.CostEstimate(
             flops=16 << 30, bytes_accessed=32 << 20, transcendentals=1 << 20
         ),
-        name="experts",
-    )(hidden, cotangent, routes, route_weight, wgu, wd, ain, aout)
+        name="whole",
+    )(queries, keys, values, hidden, cotangent, routes, route_weight, wgu, wd, ain, aout)
 
 
 def local(
     queries, keys, values, hidden, cotangent, routes, route_weight,
     w_gate_up, w_down, adapter_in, adapter_out,
 ):
-    kv = lax.all_gather(jnp.concatenate([keys, values], axis=1), "seq", axis=0, tiled=True)
-    mixed, gin, gout = experts(
-        hidden, cotangent, routes, route_weight,
+    context, mixed, gin, gout = run(
+        queries, keys, values, hidden, cotangent, routes.T, route_weight.T,
         w_gate_up[0, 0], w_down[0, 0], adapter_in[0, 0].T, adapter_out[0, 0],
     )
-    context = attend(queries, kv)
     return (context, mixed, gin.T[None, None], gout[None, None])
 
 

time: 309 us -> 259 us (0.84); the launches traced: 305 us -> 258 us
  Pallas kernels: 282 us -> 251 us
  between operations: 14.1 us -> 0.64 us
    pallas_call x2 -> x1, Pallas kernels: 282 us -> 251 us  [run(): pl.pallas_call(kernel, out_shape=(jax.ShapeDtypeStruct((TOK, HEADS * HD),...]
    unnamed x15 -> x4, local copies, waits for them, and re-layouts: 6.98 us -> 6.34 us
  transfers between devices with their start and end apart: 1 -> 0, of which waited for: 0 -> 0; matrix products, arithmetic and copies ran while one was open for 1% -> 0% of each run, Pallas kernels for 80% -> 0%
where the time goes in v2:
time: 259 us; the launch traced here: 258 us
  Pallas kernels  251 us (97%)
  local copies, waits for them, and re-layouts  6.34 us (2%)
    pallas_call x1, Pallas kernels, run(): pl.pallas_call(kernel, out_shape=(jax.ShapeDtypeStruct((TOK, HEADS * HD),...  251 us
    unnamed x4, local copies, waits for them, and re-layouts  6.34 us

profile of v2, /device:TPU:70, one launch (start us, length us, event | category | flops | bytes accessed | tf_op | source)
XLA Modules:
  0.0 258.5 jit_solution(4511629627485751322)
XLA Ops:
  0.6 251.5 %whole.1 = (bf16[128,1024]{1,0:T(8,128)(2,1)}, bf16[128,512]{1,0:T(8,128)(2,1)}, f32[16,2048]{1,0:T(8,128)}, f32[64,384]{1,0:T(8,128)}) custom-call(bf16[128,1024]{1,0:T(8,128)(2,1)} %queries.1, bf16[128,128]{1,0:T(8,128)(2,1)} %keys.1, bf16[128,128]{1,0:T(8,128)(2,1)} %values.1, bf16[128,2048]{1,0:T(8,128)(2,1)} %hid.1, bf16[128,2048]{1,0:T(8,128)(2,1)} %cot.1, ...), custom_call_target="tpu_custom_call" | custom-call | flops 17179869184 | bytes 33554432 | tf_op jit(solution)/shard_map/whole/pallas_call | solution.py:541
  252.1 1.7 copy.19
  253.8 1.6 copy.20
  255.4 1.6 copy.21
  256.9 1.5 copy.22

commit v3 on v2

v3 whole, which is shorter than its diff:
```python
import jax
import jax.numpy as jnp
from jax import lax
from jax.experimental import pallas as pl
from jax.experimental.pallas import tpu as pltpu
from jax.sharding import PartitionSpec as P

BF = jnp.bfloat16
F32 = jnp.float32
MESH = pl.DeviceIdType.MESH

TOK = 128
D = 2048
HD = 128
HEADS = 8
FF = 192
BLK = 80
MAIN = 32
ROWS = 160
NX, NZ = 4, 8
PARTS = 8
LOWR = 16
RANK = 64
KEYS = 1024
SCALE = HD**-0.5 * 1.4426950408889634
PIECES = 4
HALF = 4
OFF = (0, 2, 6, 4)


def dot(a, b, ca, cb):
    return lax.dot_general(a, b, (((ca,), (cb,)), ((), ())), preferred_element_type=F32)


def kernel(
    queries, keys, values, hid, cot, routes, rw, wgu, wd, ain, aout,
    ctx_o, mixed_o, gin_o, gout_o,
    kvb, QT, top, den, num, WG, WD, WA, WB, WBB, PL_, PR_, info, pk, tk,
    sendb, rowsb, X, C, acc, low, glow, gin, gout,
    retb, outb, gins, gouts, ginr, goutr, accm, accown, mixs, mixr, zsb, zrb,
    ws, wr, lw, was, war, rs, rr, os_, orr, gs, gr, hs, hr, ys, yr, zs, zr,
    tzs, tzr, tys, tyr, izs, izr, kzs, kzr, kxs, kxr, kcs, kcr,
):
    s = lax.axis_index("seq")
    e = lax.axis_index("ep")
    x = s // 16
    z = lax.rem(s // 2, 8)
    c = lax.rem(s, 2)
    zh = z // 4
    lz = lax.rem(z, 4)
    pair = lz // 2
    place = x * NZ + z
    mine = lz * 2 + c
    mine4 = lax.rem(lz, 2) * 2 + c

    def dev(xx, zz, cc):
        return ((xx * NZ + zz) * 2 + cc, e)

    def in_group(k):
        return dev(x, zh * 4 + k // 2, lax.rem(k, 2))

    def at_z(d):
        return dev(x, lax.rem(z + d, 8), c)

    def at_x(d):
        return dev(lax.rem(x + d, 4), z, c)

    def at_y(d):
        return (s, lax.rem(e + d, 4))

    sibling = dev(x, z, 1 - c)
    neighbour = dev(x, z + 1 - 2 * lax.rem(lz, 2), c)

    def remote(src, dst, send, recv, device):
        return pltpu.make_async_remote_copy(
            src_ref=src, dst_ref=dst, send_sem=send, recv_sem=recv, device_id=device, device_id_type=MESH
        )

    kvb[place, c, :, 0:HD] = keys[...]
    kvb[place, c, :, HD:] = values[...]
    quarter = pl.ds(pl.multiple_of(e * 32, 32), 32)
    pk[0:32] = hid[quarter, :]
    pk[32:64] = cot[quarter, :]
    lane = lax.broadcasted_iota(jnp.int32, (TOK, TOK), 1)
    sub = lax.broadcasted_iota(jnp.int32, (TOK, TOK), 0)
    ids = lax.broadcasted_iota(jnp.int32, (32, TOK), 0)
    chosen = jnp.zeros((32, TOK), F32)
    coef = jnp.zeros((32, TOK), F32)
    for j in range(8):
        hit = routes[j : j + 1, :] == ids
        chosen = chosen + jnp.where(hit, 1.0, 0.0)
        coef = coef + jnp.where(hit, rw[j : j + 1, :], 0.0)
    before = jnp.where(sub < lane, 1.0, 0.0).astype(BF)
    info[0, 0:32] = jnp.where(chosen > 0.5, dot(chosen.astype(BF), before, 1, 0), 1000.0)
    info[0, 32:64] = coef

    barrier = pltpu.get_barrier_semaphore()

    def greet(device):
        pl.semaphore_signal(barrier, inc=1, device_id=device, device_id_type=MESH)

    for d in range(1, 8):
        greet(at_z(d))
        greet(in_group(lax.rem(mine + d, 8)))
    for d in range(1, 4):
        greet(at_x(d))
        greet(at_y(d))
    pl.semaphore_wait(barrier, 20)

    def kz_copy(d):
        block = kvb.at[place, c]
        return remote(block, block, kzs.at[d - 1], kzr.at[d - 1], at_z(d))

    def kx_copy(d):
        block = kvb.at[pl.ds(x * NZ, NZ), c]
        return remote(block, block, kxs.at[d - 1], kxr.at[d - 1], at_x(d))

    def kc_copy(d):
        block = kvb.at[pl.ds(lax.rem(x + 4 - d, 4) * NZ, NZ), c]
        return remote(block, block, kcs.at[d], kcr.at[d], sibling)

    def tz_copy(j):
        return remote(pk, tk.at[j - 1, e], tzs.at[j - 1], tzr.at[j - 1], at_z(8 - OFF[j]))

    def ty_copy(j, d):
        block = tk.at[j - 1, e]
        return remote(block, block, tys.at[j - 1, d - 1], tyr.at[j - 1, d - 1], at_y(d))

    def info_copy(j):
        return remote(info.at[0], info.at[j], izs.at[j - 1], izr.at[j - 1], at_z(8 - OFF[j]))

    def slot(k, p):
        if p < 2:
            return WG.at[k, pl.ds(p * (D // 2), D // 2)]
        return (WD, WB)[p - 2].at[k]

    def own(p):
        if p < 2:
            return wgu.at[pl.ds(p * (D // 2), D // 2)]
        return (wd, aout)[p - 2]

    def w_copy(src, k, p, role, device):
        return remote(src, slot(k, p), ws.at[role, p], wr.at[k, p], device)

    def local_w(p):
        return pltpu.make_async_copy(own(p), slot(mine4, p), lw.at[p])

    def wa_copy(d):
        k = lax.rem(mine + d, 8)
        return remote(ain, WA.at[mine], was.at[d - 1], war.at[d - 1], in_group(k))

    local_wa = pltpu.make_async_copy(ain, WA.at[mine], lw.at[PIECES])
    near4 = lax.rem(mine4 + 2, 4)

    for j in (1, 2, 3):
        info_copy(j).start()
        tz_copy(j).start()
    for d in (4, 3, 5, 2, 6, 1, 7):
        kz_copy(d).start()
    for p in range(PIECES):
        w_copy(own(p), mine4, p, 0, neighbour).start()
    for p in range(PIECES):
        w_copy(own(p), mine4, p, 1, sibling).start()
        local_w(p).start()
    for d in range(1, 8):
        wa_copy(d).start()
    local_wa.start()

    row = lax.broadcasted_iota(jnp.int32, (BLK, TOK), 0)
    tail = row >= 2 * MAIN
    is_l = jnp.logical_or(row < MAIN, jnp.logical_and(tail, row < 2 * MAIN + 8))
    first = jnp.where(tail, row - MAIN, row)
    target_l = jnp.where(is_l, first, -1).astype(F32)
    target_r = jnp.where(is_l, -1, jnp.where(tail, row - MAIN - 8, row - MAIN)).astype(F32)

    def row_copy(j, n):
        return remote(sendb.at[j, n], rowsb.at[j, x], rs.at[j, n], rr.at[j, x], dev(n, z, c))

    def dispatch(j, h, g):
        @pl.loop(0, NX)
        def _(n):
            expert = e * 8 + n * 2 + zh
            slots = info[j, pl.ds(expert, 1), :]
            p_l = jnp.where(slots == target_l, 1.0, 0.0)
            p_r = jnp.where(slots == target_r, 1.0, 0.0)
            coef_r = jnp.sum(p_r * info[j, pl.ds(32 + expert, 1), :], axis=1, keepdims=True)
            p_l = p_l.astype(BF)
            p_r = p_r.astype(BF)
            PL_[j, n] = p_l
            PR_[j, n] = p_r
            block = (dot(p_l, h(), 1, 0) + dot(p_r, g(), 1, 0) * coef_r).astype(BF)

            @pl.when(n == x)
            def _():
                rowsb[j, n] = block

            @pl.when(n != x)
            def _():
                sendb[j, n] = block
                row_copy(j, n).start()

    dispatch(0, lambda: hid[...], lambda: cot[...])

    for j in (1, 2, 3):
        tz_copy(j).wait_recv()
        for d in (2, 1, 3):
            ty_copy(j, d).start()
    for d in range(1, 8):
        kz_copy(d).wait_recv()
    for d in (2, 1, 3):
        kx_copy(d).start()
    kc_copy(0).start()
    for h in range(HEADS):
        QT[h] = queries[:, h * HD : (h + 1) * HD].astype(F32).T.astype(BF)
    top[...] = jnp.full_like(top, -1e30)
    den[...] = jnp.zeros_like(den)
    num[...] = jnp.zeros_like(num)
    gin[...] = jnp.zeros_like(gin)
    gout[...] = jnp.zeros_like(gout)

    for j in (1, 2, 3):
        info_copy(j).wait_recv()

    @pl.loop(1, 4)
    def _(j):
        for d in (1, 3, 2):
            block = tk.at[j - 1, e]
            remote(block, block, tys.at[j - 1, d - 1], tyr.at[j - 1, d - 1], sibling).wait_recv()
        dispatch(
            j,
            lambda: tk[j - 1, :, 0:32].reshape(TOK, D),
            lambda: tk[j - 1, :, 32:64].reshape(TOK, D),
        )

    for d in (1, 3, 2):
        kx_copy(d).wait_recv()
        kc_copy(d).start()
    for d in range(4):
        kc_copy(d).wait_recv()

    def absorb(block, masked):
        kv = kvb[pl.ds(block * (KEYS // 256), KEYS // 256)]
        ks = kv[..., :HD].reshape(KEYS, HD)
        vs = kv[..., HD:].reshape(KEYS, HD)
        if masked:
            kpos = block * KEYS + lax.broadcasted_iota(jnp.int32, (KEYS, TOK), 0)
            qpos = s * TOK + lax.broadcasted_iota(jnp.int32, (KEYS, TOK), 1)
            allowed = kpos <= qpos
        for h in range(HEADS):
            sc = dot(ks, QT[h], 1, 0)
            if masked:
                sc = jnp.where(allowed, sc, -1e30)
            old = top[h, 0:1]
            new = jnp.maximum(old, jnp.max(sc, axis=0, keepdims=True))
            factor = jnp.exp2((old - new) * SCALE)
            w = jnp.exp2((sc - new) * SCALE)
            den[h, 0:1] = den[h, 0:1] * factor + jnp.sum(w, axis=0, keepdims=True)
            num[h] = num[h] * factor + dot(vs, w.astype(BF), 0, 0)
            top[h, 0:1] = new

    full = s // (KEYS // TOK)

    @pl.loop(0, full)
    def _(t):
        absorb(t, False)

    absorb(full, True)
    for h in range(HEADS):
        ctx_o[:, h * HD : (h + 1) * HD] = (num[h] / den[h, 0:1]).T.astype(BF)

    for p in range(PIECES):
        w_copy(slot(near4, p), near4, p, 0, sibling).wait_recv()
        w_copy(slot(near4, p), near4, p, 2, sibling).start()
    for d in range(1, 8):
        wa_copy(d).wait_recv()
    local_wa.wait()
    for p in range(PIECES):
        local_w(p).wait()
        for l in range(2):
            k = 2 * l + 1 - c
            w_copy(slot(k, p), k, p, 0, sibling).wait_recv()

    lanes = lax.broadcasted_iota(jnp.int32, (RANK, 2 * FF), 1)

    @pl.loop(0, HALF)
    def _(k):
        b = WB[k].astype(F32)
        WBB[k, pl.ds(0, RANK)] = jnp.where(lanes < FF, b, 0.0).astype(BF)
        WBB[k, pl.ds(RANK, RANK)] = jnp.where(lanes >= FF, b, 0.0).astype(BF)

    def work(i):
        for j in range(4):
            X[j * MAIN : (j + 1) * MAIN] = rowsb[i, j, 0:MAIN]
            C[j * MAIN : (j + 1) * MAIN] = rowsb[i, j, MAIN : 2 * MAIN]
        for j in range(2):
            t0 = rowsb[i, 2 * j, 2 * MAIN : BLK].astype(F32)
            t1 = rowsb[i, 2 * j + 1, 2 * MAIN : BLK].astype(F32)
            at = 4 * MAIN + 16 * j
            X[at : at + 16] = jnp.concatenate([t0[:8], t1[:8]], axis=0).astype(BF)
            C[at : at + 16] = jnp.concatenate([t0[8:], t1[8:]], axis=0).astype(BF)
        low[...] = dot(X[...], WA[...].reshape(PARTS * LOWR, D), 1, 1).astype(BF)
        glow[...] = jnp.zeros_like(glow)
        acc[...] = jnp.zeros_like(acc)

        @pl.loop(0, HALF)
        def _(k):
            lo = low[...]
            pre = dot(X[...], WG[k], 1, 0) + dot(lo, WBB[k], 1, 0)
            g = pre[:, :FF]
            u = pre[:, FF:]
            back = dot(C[...], WD[k], 1, 1)
            sig = 1.0 / (1.0 + jnp.exp(-g))
            silu = g * sig
            acc[...] += dot((silu * u).astype(BF), WD[k], 1, 0)
            dg = back * u * sig * (1.0 + g * (1.0 - sig))
            du = back * silu
            dgu = jnp.concatenate([dg, du], axis=1).astype(BF)
            r = dot(lo, dgu, 0, 0)
            gout[k] += jnp.where(lanes < FF, r[:RANK], r[RANK:])
            glow[...] += dot(dgu, WBB[k], 1, 1)

        for j in range(4):
            a = acc[j * MAIN : (j + 1) * MAIN].astype(BF)
            t = acc[4 * MAIN + 8 * j : 4 * MAIN + 8 * j + 8]
            t = jnp.concatenate([t[:, : D // 2], t[:, D // 2 :]], axis=0).astype(BF)

            @pl.when(x == j)
            def _():
                outb[i, j, 0:MAIN] = a[:, : D // 2]
                outb[i, j, MAIN : 2 * MAIN] = a[:, D // 2 :]
                outb[i, j, 2 * MAIN : BLK] = t

            @pl.when(x != j)
            def _():
                retb[i, j, 0:MAIN] = a[:, : D // 2]
                retb[i, j, MAIN : 2 * MAIN] = a[:, D // 2 :]
                retb[i, j, 2 * MAIN : BLK] = t
                remote(retb.at[i, j], outb.at[i, x], os_.at[i, j], orr.at[i, x], dev(j, z, c)).start()

        gin[...] += dot(glow[...].astype(BF), X[...], 0, 0)

    eye = sub == lane

    def y_copy(j, d):
        to = lax.rem(e + d, 4)
        return remote(mixs.at[j, to], mixr.at[j, d - 1], ys.at[j, d - 1], yr.at[j, d - 1], at_y(d))

    def combine(j):
        accm[...] = jnp.zeros_like(accm)

        @pl.loop(0, NX)
        def _(n):
            @pl.when(n != x)
            def _():
                remote(outb.at[j, n], outb.at[j, n], os_.at[j, 0], orr.at[j, n], sibling).wait_recv()

            coefs = info[j, pl.ds(32 + e * 8 + n * 2 + zh, 1), :]
            cf = jnp.sum(jnp.where(eye, coefs, 0.0), axis=1, keepdims=True)
            block = outb[j, n]
            accm[:, : D // 2] += cf * dot(PL_[j, n], block, 0, 0)
            accm[:, D // 2 :] += cf * dot(PR_[j, n], block, 0, 0)

        for yy in range(4):
            mixs[j, yy] = accm[:, yy * 512 : (yy + 1) * 512].astype(BF)
        for d in (2, 1, 3):
            y_copy(j, d).start()
        accown[j] = accm[:, pl.ds(pl.multiple_of(e * 512, 512), 512)]

    def home_copy(j, device):
        return remote(zsb.at[j - 1], zrb.at[j - 1], zs.at[j - 1], zr.at[j - 1], device)

    def send_home(j):
        for d in (1, 3, 2):
            y_copy(j, d).wait_recv()
        total = accown[j]
        for d in range(3):
            total = total + mixr[j, d].astype(F32)

        @pl.when(j == 0)
        def _():
            accown[0] = total

        @pl.when(j > 0)
        def _():
            zsb[j - 1] = total.astype(BF)
            home_copy(j, at_z(jnp.where(j == 3, 4, jnp.where(j == 2, 6, 2)))).start()

    @pl.loop(0, 4)
    def _(j):
        @pl.loop(0, NX)
        def _(n):
            @pl.when(n != x)
            def _():
                remote(rowsb.at[j, n], rowsb.at[j, n], rs.at[j, 0], rr.at[j, n], sibling).wait_recv()

        work(j)

        @pl.when(j >= 1)
        def _():
            combine(j - 1)

        @pl.when(j >= 2)
        def _():
            send_home(j - 2)

    gins[...] = gin[...].reshape(PARTS, LOWR, D).astype(BF)
    gouts[...] = gout[...].astype(BF)

    def gin_copy(d):
        k = lax.rem(mine + d, 8)
        return remote(gins.at[k], ginr.at[d - 1], gs.at[d - 1], gr.at[d - 1], in_group(k))

    def gout_copy(d):
        k = lax.rem(mine4 + d, 4)
        return remote(gouts.at[k], goutr.at[d - 1], hs.at[d - 1], hr.at[d - 1], in_group(pair * 4 + k))

    for d in range(1, 8):
        gin_copy(d).start()
    for d in range(1, 4):
        gout_copy(d).start()

    combine(3)
    send_home(2)
    send_home(3)

    for d in range(1, 8):
        gin_copy(d).wait_recv()
    for d in range(1, 4):
        gout_copy(d).wait_recv()
    total = gins[mine].astype(F32)
    for d in range(7):
        total = total + ginr[d].astype(F32)
    gin_o[...] = total
    total = gout[mine4]
    for d in range(3):
        total = total + goutr[d].astype(F32)
    gout_o[...] = total

    total = accown[0]
    for j in (1, 2, 3):
        home_copy(j, sibling).wait_recv()
        total = total + zrb[j - 1].astype(F32)
    mixed_o[...] = total.astype(BF)

    for j in (1, 2, 3):
        info_copy(j).wait_send()
        tz_copy(j).wait_send()
        home_copy(j, sibling).wait_send()
        for d in range(1, 4):
            ty_copy(j, d).wait_send()
    for d in range(1, 8):
        kz_copy(d).wait_send()
        wa_copy(d).wait_send()
        gin_copy(d).wait_send()
    for d in range(1, 4):
        kx_copy(d).wait_send()
        gout_copy(d).wait_send()
    for d in range(4):
        kc_copy(d).wait_send()
    for p in range(PIECES):
        w_copy(own(p), mine4, p, 0, neighbour).wait_send()
        w_copy(own(p), mine4, p, 1, sibling).wait_send()
        w_copy(slot(near4, p), near4, p, 2, sibling).wait_send()

    @pl.loop(0, 4)
    def _(j):
        for d in range(1, 4):
            y_copy(j, d).wait_send()

        @pl.loop(0, NX)
        def _(n):
            @pl.when(n != x)
            def _():
                row_copy(j, n).wait_send()
                remote(retb.at[j, n], outb.at[j, x], os_.at[j, n], orr.at[j, x], sibling).wait_send()


def run(queries, keys, values, hidden, cotangent, routes, route_weight, wgu, wd, ain, aout):
    vm = pl.BlockSpec(memory_space=pltpu.VMEM)
    hbm = pl.BlockSpec(memory_space=pl.ANY)
    dma = pltpu.SemaphoreType.DMA
    v = pltpu.VMEM
    return pl.pallas_call(
        kernel,
        out_shape=(
            jax.ShapeDtypeStruct((TOK, HEADS * HD), BF),
            jax.ShapeDtypeStruct((TOK, 512), BF),
            jax.ShapeDtypeStruct((LOWR, D), F32),
            jax.ShapeDtypeStruct((RANK, 2 * FF), F32),
        ),
        in_specs=[vm] * 7 + [hbm] * 4,
        out_specs=(vm,) * 4,
        scratch_shapes=[
            v((NX * NZ, 2, TOK, 2 * HD), BF),
            v((HEADS, HD, TOK), BF),
            v((HEADS, 8, TOK), F32),
            v((HEADS, 8, TOK), F32),
            v((HEADS, HD, TOK), F32),
            v((HALF, D, 2 * FF), BF),
            v((HALF, FF, D), BF),
            v((PARTS, LOWR, D), BF),
            v((HALF, RANK, 2 * FF), BF),
            v((HALF, 2 * RANK, 2 * FF), BF),
            v((4, NX, BLK, TOK), BF),
            v((4, NX, BLK, TOK), BF),
            v((4, 64, TOK), F32),
            v((64, D), BF),
            v((3, 4, 64, D), BF),
            v((4, NX, BLK, D), BF),
            v((4, NX, BLK, D), BF),
            v((ROWS, D), BF),
            v((ROWS, D), BF),
            v((ROWS, D), F32),
            v((ROWS, 2 * RANK), BF),
            v((ROWS, 2 * RANK), F32),
            v((PARTS * LOWR, D), F32),
            v((HALF, RANK, 2 * FF), F32),
            v((4, NX, BLK, D // 2), BF),
            v((4, NX, BLK, D // 2), BF),
            v((PARTS, LOWR, D), BF),
            v((HALF, RANK, 2 * FF), BF),
            v((7, LOWR, D), BF),
            v((3, RANK, 2 * FF), BF),
            v((TOK, D), F32),
            v((4, TOK, 512), F32),
            v((4, 4, TOK, 512), BF),
            v((4, 3, TOK, 512), BF),
            v((3, TOK, 512), BF),
            v((3, TOK, 512), BF),
            dma((3, PIECES)),
            dma((HALF, PIECES)),
            dma((PIECES + 1,)),
            dma((7,)),
            dma((7,)),
            dma((4, NX)),
            dma((4, NX)),
            dma((4, NX)),
            dma((4, NX)),
            dma((7,)),
            dma((7,)),
            dma((3,)),
            dma((3,)),
            dma((4, 3)),
            dma((4, 3)),
            dma((3,)),
            dma((3,)),
            dma((3,)),
            dma((3,)),
            dma((3, 3)),
            dma((3, 3)),
            dma((3,)),
            dma((3,)),
            dma((7,)),
            dma((7,)),
            dma((3,)),
            dma((3,)),
            dma((4,)),
            dma((4,)),
        ],
        compiler_params=pltpu.CompilerParams(
            collective_id=0, has_side_effects=True, vmem_limit_bytes=60 << 20
        ),
        cost_estimate=pl.CostEstimate(
            flops=16 << 30, bytes_accessed=32 << 20, transcendentals=8 << 20
        ),
        name="whole",
    )(queries, keys, values, hidden, cotangent, routes, route_weight, wgu, wd, ain, aout)


def local(
    queries, keys, values, hidden, cotangent, routes, route_weight,
    w_gate_up, w_down, adapter_in, adapter_out,
):
    context, mixed, gin, gout = run(
        queries, keys, values, hidden, cotangent, routes.T, route_weight.T,
        w_gate_up[0, 0], w_down[0, 0], adapter_in[0, 0].T, adapter_out[0, 0],
    )
    return (context, mixed, gin.T[None, None], gout[None, None])


def solution(mesh):
    return jax.shard_map(
        local,
        mesh=mesh,
        in_specs=(
            P("seq", "ep"),
            P("seq", "ep"),
            P("seq", "ep"),
            P("seq", None),
            P("seq", None),
            P("seq", None),
            P("seq", None),
            P("ep", "seq", None, None),
            P("ep", "seq", None, None),
            P("ep", "seq", None, None),
            P("ep", "seq", None, None),
        ),
        out_specs=(
            P("seq", "ep"),
            P("seq", "ep"),
            P("ep", "seq", None, None),
            P("ep", "seq", None, None),
        ),
        check_vma=False,
    )
```

time: 259 us -> 176 us (0.68)
  the two profiles are of different devices: /device:TPU:70 before, /device:TPU:1 now
where the time goes in v3:
time: 176 us
  Pallas kernels  169 us (96%)
  local copies, waits for them, and re-layouts  6.34 us (4%)
    pallas_call x1, Pallas kernels, run(): pl.pallas_call(kernel, out_shape=(jax.ShapeDtypeStruct((TOK, HEADS * HD),...  169 us
    unnamed x4, local copies, waits for them, and re-layouts  6.34 us

profile of v3, /device:TPU:1, one launch (start us, length us, event | category | flops | bytes accessed | tf_op | source)
XLA Modules:
  0.0 175.6 jit_solution(11791787850578499569)
XLA Ops:
  0.6 168.6 %whole.1 = (bf16[128,1024]{1,0:T(8,128)(2,1)}, bf16[128,512]{1,0:T(8,128)(2,1)}, f32[16,2048]{1,0:T(8,128)}, f32[64,384]{1,0:T(8,128)}) custom-call(bf16[128,1024]{1,0:T(8,128)(2,1)} %queries.1, bf16[128,128]{1,0:T(8,128)(2,1)} %keys.1, bf16[128,128]{1,0:T(8,128)(2,1)} %values.1, bf16[128,2048]{1,0:T(8,128)(2,1)} %hid.1, bf16[128,2048]{1,0:T(8,128)(2,1)} %cot.1, ...), custom_call_target="tpu_custom_call" | custom-call | flops 17179869184 | bytes 33554432 | tf_op jit(solution)/shard_map/whole/pallas_call | solution.py:483
  169.3 1.7 copy.19
  171.0 1.6 copy.20
  172.5 1.6 copy.21
  174.1 1.5 copy.22

commit v4 on v3

--- a/solution.py
+++ b/solution.py
@@ -35,9 +35,9 @@
 def kernel(
     queries, keys, values, hid, cot, routes, rw, wgu, wd, ain, aout,
     ctx_o, mixed_o, gin_o, gout_o,
-    kvb, QT, top, den, num, WG, WD, WA, WB, WBB, PL_, PR_, info, pk, tk,
+    kvb, QT, top, den, num, WG, WD, WA, WB, WBB, PA, PL_, PR_, info, sl2, tk,
     sendb, rowsb, X, C, acc, low, glow, gin, gout,
-    retb, outb, gins, gouts, ginr, goutr, accm, accown, mixs, mixr, zsb, zrb,
+    retb, outb, gins, gouts, ginr, goutr, accown, mixs, mixr, zsb, zrb,
     ws, wr, lw, was, war, rs, rr, os_, orr, gs, gr, hs, hr, ys, yr, zs, zr,
     tzs, tzr, tys, tyr, izs, izr, kzs, kzr, kxs, kxr, kcs, kcr,
 ):
@@ -78,9 +78,9 @@
 
     kvb[place, c, :, 0:HD] = keys[...]
     kvb[place, c, :, HD:] = values[...]
-    quarter = pl.ds(pl.multiple_of(e * 32, 32), 32)
-    pk[0:32] = hid[quarter, :]
-    pk[32:64] = cot[quarter, :]
+    for j in range(4):
+        tk[0, j, 0:32] = hid[j * 32 : (j + 1) * 32]
+        tk[0, j, 32:64] = cot[j * 32 : (j + 1) * 32]
     lane = lax.broadcasted_iota(jnp.int32, (TOK, TOK), 1)
     sub = lax.broadcasted_iota(jnp.int32, (TOK, TOK), 0)
     ids = lax.broadcasted_iota(jnp.int32, (32, TOK), 0)
@@ -91,7 +91,7 @@
         chosen = chosen + jnp.where(hit, 1.0, 0.0)
         coef = coef + jnp.where(hit, rw[j : j + 1, :], 0.0)
     before = jnp.where(sub < lane, 1.0, 0.0).astype(BF)
-    info[0, 0:32] = jnp.where(chosen > 0.5, dot(chosen.astype(BF), before, 1, 0), 1000.0)
+    info[0, 0:32] = jnp.where(chosen > 0.5, dot(chosen.astype(BF), before, 1, 0), 512.0)
     info[0, 32:64] = coef
 
     barrier = pltpu.get_barrier_semaphore()
@@ -120,10 +120,10 @@
         return remote(block, block, kcs.at[d], kcr.at[d], sibling)
 
     def tz_copy(j):
-        return remote(pk, tk.at[j - 1, e], tzs.at[j - 1], tzr.at[j - 1], at_z(8 - OFF[j]))
+        return remote(tk.at[0, e], tk.at[j, e], tzs.at[j - 1], tzr.at[j - 1], at_z(8 - OFF[j]))
 
     def ty_copy(j, d):
-        block = tk.at[j - 1, e]
+        block = tk.at[j, e]
         return remote(block, block, tys.at[j - 1, d - 1], tyr.at[j - 1, d - 1], at_y(d))
 
     def info_copy(j):
@@ -152,91 +152,114 @@
     local_wa = pltpu.make_async_copy(ain, WA.at[mine], lw.at[PIECES])
     near4 = lax.rem(mine4 + 2, 4)
 
-    for j in (1, 2, 3):
+    for j in (1, 2):
         info_copy(j).start()
         tz_copy(j).start()
-    for d in (4, 3, 5, 2, 6, 1, 7):
-        kz_copy(d).start()
-    for p in range(PIECES):
-        w_copy(own(p), mine4, p, 0, neighbour).start()
     for p in range(PIECES):
         w_copy(own(p), mine4, p, 1, sibling).start()
         local_w(p).start()
-    for d in range(1, 8):
-        wa_copy(d).start()
     local_wa.start()
 
-    row = lax.broadcasted_iota(jnp.int32, (BLK, TOK), 0)
+    row = lax.broadcasted_iota(jnp.int32, (BLK, 2 * TOK), 0)
     tail = row >= 2 * MAIN
     is_l = jnp.logical_or(row < MAIN, jnp.logical_and(tail, row < 2 * MAIN + 8))
-    first = jnp.where(tail, row - MAIN, row)
-    target_l = jnp.where(is_l, first, -1).astype(F32)
-    target_r = jnp.where(is_l, -1, jnp.where(tail, row - MAIN - 8, row - MAIN)).astype(F32)
+    first = jnp.where(tail, row - MAIN, row).astype(F32)
+    second = jnp.where(tail, row - MAIN - 8, row - MAIN).astype(F32)
+    target_l = jnp.where(is_l, first, -1.0)
+    target_r = jnp.where(is_l, -1.0, second)
+    one_l = jnp.where(is_l, 1.0, 0.0)[:, :1]
+    wide = lax.broadcasted_iota(jnp.int32, (BLK, 2 * TOK), 1)
+    target_w = jnp.where(lax.rem(wide, 64) < 32, target_l, target_r)
+    target_l = target_l[:, :TOK]
+    target_r = target_r[:, :TOK]
+    wide = lax.broadcasted_iota(jnp.int32, (TOK, 2 * TOK), 1)
+    token = lax.broadcasted_iota(jnp.int32, (TOK, 2 * TOK), 0)
+    spread = jnp.where((wide // 64) * 32 + lax.rem(wide, 32) == token, 1.0, 0.0).astype(BF)
 
     def row_copy(j, n):
         return remote(sendb.at[j, n], rowsb.at[j, x], rs.at[j, n], rr.at[j, x], dev(n, z, c))
 
-    def dispatch(j, h, g):
+    def dispatch(j):
+        sl2[...] = dot(info[j, 0:32].astype(BF), spread, 1, 0)
+        factor = []
+        for n in range(NX):
+            expert = e * 8 + n * 2 + zh
+            slots = info[j, pl.ds(expert, 1), :]
+            coefs = info[j, pl.ds(32 + expert, 1), :]
+            p_l = jnp.where(slots == target_l, coefs, 0.0)
+            p_r = jnp.where(slots == target_r, coefs, 0.0)
+            factor.append(jnp.sum(p_r, axis=1, keepdims=True) + one_l)
+            PL_[j, n] = p_l.astype(BF)
+            PR_[j, n] = p_r.astype(BF)
+            PA[n] = jnp.where(sl2[pl.ds(expert, 1), :] == target_w, 1.0, 0.0).astype(BF)
+        for half in range(2):
+            cols = slice(half * (D // 2), (half + 1) * (D // 2))
+            picked = dot(PA[...].reshape(NX * BLK, 2 * TOK), tk[j, :, :, cols].reshape(2 * TOK, D // 2), 1, 0)
+            for n in range(NX):
+                block = (picked[n * BLK : (n + 1) * BLK] * factor[n]).astype(BF)
+
+                @pl.when(n == x)
+                def _():
+                    rowsb[j, n, :, cols] = block
+
+                @pl.when(n != x)
+                def _():
+                    sendb[j, n, :, cols] = block
+
         @pl.loop(0, NX)
         def _(n):
-            expert = e * 8 + n * 2 + zh
-            slots = info[j, pl.ds(expert, 1), :]
-            p_l = jnp.where(slots == target_l, 1.0, 0.0)
-            p_r = jnp.where(slots == target_r, 1.0, 0.0)
-            coef_r = jnp.sum(p_r * info[j, pl.ds(32 + expert, 1), :], axis=1, keepdims=True)
-            p_l = p_l.astype(BF)
-            p_r = p_r.astype(BF)
-            PL_[j, n] = p_l
-            PR_[j, n] = p_r
-            block = (dot(p_l, h(), 1, 0) + dot(p_r, g(), 1, 0) * coef_r).astype(BF)
-
-            @pl.when(n == x)
-            def _():
-                rowsb[j, n] = block
-
             @pl.when(n != x)
             def _():
-                sendb[j, n] = block
                 row_copy(j, n).start()
 
-    dispatch(0, lambda: hid[...], lambda: cot[...])
-
-    for j in (1, 2, 3):
-        tz_copy(j).wait_recv()
+    def from_z(j):
+        remote(tk.at[j, e], tk.at[j, e], tzs.at[j - 1], tzr.at[j - 1], sibling).wait_recv()
+        remote(info.at[j], info.at[j], izs.at[j - 1], izr.at[j - 1], sibling).wait_recv()
         for d in (2, 1, 3):
             ty_copy(j, d).start()
-    for d in range(1, 8):
-        kz_copy(d).wait_recv()
-    for d in (2, 1, 3):
-        kx_copy(d).start()
-    kc_copy(0).start()
+
+    def more_sends():
+        info_copy(3).start()
+        tz_copy(3).start()
+        for d in range(1, 8):
+            wa_copy(d).start()
+        for d in (4, 3, 5, 2, 6, 1, 7):
+            kz_copy(d).start()
+        for p in range(PIECES):
+            w_copy(own(p), mine4, p, 0, neighbour).start()
+
+    @pl.loop(0, 4)
+    def _(j):
+        @pl.when(j >= 1)
+        def _():
+            for d in (1, 3, 2):
+                ty_copy(j, d).wait_recv()
+
+            @pl.when(j < 3)
+            def _():
+                from_z(j + 1)
+
+        dispatch(j)
+
+        @pl.when(j == 0)
+        def _():
+            more_sends()
+            from_z(1)
+
+        @pl.when(j == 3)
+        def _():
+            for d in range(1, 8):
+                kz_copy(d).wait_recv()
+            for d in (2, 1, 3):
+                kx_copy(d).start()
+            kc_copy(0).start()
+
     for h in range(HEADS):
         QT[h] = queries[:, h * HD : (h + 1) * HD].astype(F32).T.astype(BF)
     top[...] = jnp.full_like(top, -1e30)
     den[...] = jnp.zeros_like(den)
     num[...] = jnp.zeros_like(num)
-    gin[...] = jnp.zeros_like(gin)
     gout[...] = jnp.zeros_like(gout)
-
-    for j in (1, 2, 3):
-        info_copy(j).wait_recv()
-
-    @pl.loop(1, 4)
-    def _(j):
-        for d in (1, 3, 2):
-            block = tk.at[j - 1, e]
-            remote(block, block, tys.at[j - 1, d - 1], tyr.at[j - 1, d - 1], sibling).wait_recv()
-        dispatch(
-            j,
-            lambda: tk[j - 1, :, 0:32].reshape(TOK, D),
-            lambda: tk[j - 1, :, 32:64].reshape(TOK, D),
-        )
-
-    for d in (1, 3, 2):
-        kx_copy(d).wait_recv()
-        kc_copy(d).start()
-    for d in range(4):
-        kc_copy(d).wait_recv()
 
     def absorb(block, masked):
         kv = kvb[pl.ds(block * (KEYS // 256), KEYS // 256)]
@@ -260,68 +283,49 @@
 
     full = s // (KEYS // TOK)
 
-    @pl.loop(0, full)
-    def _(t):
-        absorb(t, False)
-
-    absorb(full, True)
-    for h in range(HEADS):
-        ctx_o[:, h * HD : (h + 1) * HD] = (num[h] / den[h, 0:1]).T.astype(BF)
-
-    for p in range(PIECES):
-        w_copy(slot(near4, p), near4, p, 0, sibling).wait_recv()
-        w_copy(slot(near4, p), near4, p, 2, sibling).start()
-    for d in range(1, 8):
-        wa_copy(d).wait_recv()
-    local_wa.wait()
-    for p in range(PIECES):
-        local_w(p).wait()
-        for l in range(2):
-            k = 2 * l + 1 - c
-            w_copy(slot(k, p), k, p, 0, sibling).wait_recv()
-
     lanes = lax.broadcasted_iota(jnp.int32, (RANK, 2 * FF), 1)
 
-    @pl.loop(0, HALF)
-    def _(k):
+    def spread_wb(k):
         b = WB[k].astype(F32)
         WBB[k, pl.ds(0, RANK)] = jnp.where(lanes < FF, b, 0.0).astype(BF)
         WBB[k, pl.ds(RANK, RANK)] = jnp.where(lanes >= FF, b, 0.0).astype(BF)
 
-    def work(i):
+    def prepare(i):
         for j in range(4):
-            X[j * MAIN : (j + 1) * MAIN] = rowsb[i, j, 0:MAIN]
-            C[j * MAIN : (j + 1) * MAIN] = rowsb[i, j, MAIN : 2 * MAIN]
+            X[i, j * MAIN : (j + 1) * MAIN] = rowsb[i, j, 0:MAIN]
+            C[i, j * MAIN : (j + 1) * MAIN] = rowsb[i, j, MAIN : 2 * MAIN]
         for j in range(2):
             t0 = rowsb[i, 2 * j, 2 * MAIN : BLK].astype(F32)
             t1 = rowsb[i, 2 * j + 1, 2 * MAIN : BLK].astype(F32)
             at = 4 * MAIN + 16 * j
-            X[at : at + 16] = jnp.concatenate([t0[:8], t1[:8]], axis=0).astype(BF)
-            C[at : at + 16] = jnp.concatenate([t0[8:], t1[8:]], axis=0).astype(BF)
-        low[...] = dot(X[...], WA[...].reshape(PARTS * LOWR, D), 1, 1).astype(BF)
-        glow[...] = jnp.zeros_like(glow)
-        acc[...] = jnp.zeros_like(acc)
-
-        @pl.loop(0, HALF)
+            X[i, at : at + 16] = jnp.concatenate([t0[:8], t1[:8]], axis=0).astype(BF)
+            C[i, at : at + 16] = jnp.concatenate([t0[8:], t1[8:]], axis=0).astype(BF)
+        low[i] = dot(X[i], WA[...].reshape(PARTS * LOWR, D), 1, 1).astype(BF)
+        glow[i] = jnp.zeros((ROWS, 2 * RANK), F32)
+        acc[i] = jnp.zeros((ROWS, D), F32)
+
+    def parts(i, base):
+        @pl.loop(base, base + 2)
         def _(k):
-            lo = low[...]
-            pre = dot(X[...], WG[k], 1, 0) + dot(lo, WBB[k], 1, 0)
+            lo = low[i]
+            pre = dot(X[i], WG[k], 1, 0) + dot(lo, WBB[k], 1, 0)
             g = pre[:, :FF]
             u = pre[:, FF:]
-            back = dot(C[...], WD[k], 1, 1)
+            back = dot(C[i], WD[k], 1, 1)
             sig = 1.0 / (1.0 + jnp.exp(-g))
             silu = g * sig
-            acc[...] += dot((silu * u).astype(BF), WD[k], 1, 0)
+            acc[i] += dot((silu * u).astype(BF), WD[k], 1, 0)
             dg = back * u * sig * (1.0 + g * (1.0 - sig))
             du = back * silu
             dgu = jnp.concatenate([dg, du], axis=1).astype(BF)
             r = dot(lo, dgu, 0, 0)
             gout[k] += jnp.where(lanes < FF, r[:RANK], r[RANK:])
-            glow[...] += dot(dgu, WBB[k], 1, 1)
-
+            glow[i] += dot(dgu, WBB[k], 1, 1)
+
+    def give_back(i):
         for j in range(4):
-            a = acc[j * MAIN : (j + 1) * MAIN].astype(BF)
-            t = acc[4 * MAIN + 8 * j : 4 * MAIN + 8 * j + 8]
+            a = acc[i, j * MAIN : (j + 1) * MAIN].astype(BF)
+            t = acc[i, 4 * MAIN + 8 * j : 4 * MAIN + 8 * j + 8]
             t = jnp.concatenate([t[:, : D // 2], t[:, D // 2 :]], axis=0).astype(BF)
 
             @pl.when(x == j)
@@ -337,34 +341,24 @@
                 retb[i, j, 2 * MAIN : BLK] = t
                 remote(retb.at[i, j], outb.at[i, x], os_.at[i, j], orr.at[i, x], dev(j, z, c)).start()
 
-        gin[...] += dot(glow[...].astype(BF), X[...], 0, 0)
-
-    eye = sub == lane
 
     def y_copy(j, d):
         to = lax.rem(e + d, 4)
         return remote(mixs.at[j, to], mixr.at[j, d - 1], ys.at[j, d - 1], yr.at[j, d - 1], at_y(d))
 
     def combine(j):
-        accm[...] = jnp.zeros_like(accm)
-
         @pl.loop(0, NX)
         def _(n):
             @pl.when(n != x)
             def _():
                 remote(outb.at[j, n], outb.at[j, n], os_.at[j, 0], orr.at[j, n], sibling).wait_recv()
 
-            coefs = info[j, pl.ds(32 + e * 8 + n * 2 + zh, 1), :]
-            cf = jnp.sum(jnp.where(eye, coefs, 0.0), axis=1, keepdims=True)
-            block = outb[j, n]
-            accm[:, : D // 2] += cf * dot(PL_[j, n], block, 0, 0)
-            accm[:, D // 2 :] += cf * dot(PR_[j, n], block, 0, 0)
-
-        for yy in range(4):
-            mixs[j, yy] = accm[:, yy * 512 : (yy + 1) * 512].astype(BF)
+        for i, p in enumerate((PL_, PR_)):
+            part = dot(p[j].reshape(NX * BLK, TOK), outb[j].reshape(NX * BLK, D // 2), 0, 0).astype(BF)
+            mixs[j, 2 * i] = part[:, :512]
+            mixs[j, 2 * i + 1] = part[:, 512:]
         for d in (2, 1, 3):
             y_copy(j, d).start()
-        accown[j] = accm[:, pl.ds(pl.multiple_of(e * 512, 512), 512)]
 
     def home_copy(j, device):
         return remote(zsb.at[j - 1], zrb.at[j - 1], zs.at[j - 1], zr.at[j - 1], device)
@@ -372,18 +366,31 @@
     def send_home(j):
         for d in (1, 3, 2):
             y_copy(j, d).wait_recv()
-        total = accown[j]
+        total = mixs[j, e].astype(F32)
         for d in range(3):
             total = total + mixr[j, d].astype(F32)
 
         @pl.when(j == 0)
         def _():
-            accown[0] = total
+            accown[...] = total
 
         @pl.when(j > 0)
         def _():
             zsb[j - 1] = total.astype(BF)
             home_copy(j, at_z(jnp.where(j == 3, 4, jnp.where(j == 2, 6, 2)))).start()
+
+    here = lax.rem(lz, 2) * 2
+    there = 2 - here
+    for p in range(PIECES):
+        local_w(p).wait()
+        w_copy(slot(here + 1 - c, p), here + 1 - c, p, 0, sibling).wait_recv()
+    local_wa.wait()
+    for d in range(1, 8):
+        wa_copy(d).wait_recv()
+
+    @pl.loop(here, here + 2)
+    def _(k):
+        spread_wb(k)
 
     @pl.loop(0, 4)
     def _(j):
@@ -393,15 +400,26 @@
             def _():
                 remote(rowsb.at[j, n], rowsb.at[j, n], rs.at[j, 0], rr.at[j, n], sibling).wait_recv()
 
-        work(j)
-
-        @pl.when(j >= 1)
-        def _():
-            combine(j - 1)
-
-        @pl.when(j >= 2)
-        def _():
-            send_home(j - 2)
+        prepare(j)
+        parts(j, here)
+
+    for p in range(PIECES):
+        w_copy(slot(near4, p), near4, p, 0, sibling).wait_recv()
+        w_copy(slot(near4, p), near4, p, 2, sibling).start()
+    for p in range(PIECES):
+        w_copy(slot(there + 1 - c, p), there + 1 - c, p, 0, sibling).wait_recv()
+
+    @pl.loop(there, there + 2)
+    def _(k):
+        spread_wb(k)
+
+    @pl.loop(1, 5)
+    def _(jj):
+        j = lax.rem(jj, 4)
+        parts(j, there)
+        give_back(j)
+
+    gin[...] = dot(glow[...].reshape(4 * ROWS, 2 * RANK).astype(BF), X[...].reshape(4 * ROWS, D), 0, 0)
 
     gins[...] = gin[...].reshape(PARTS, LOWR, D).astype(BF)
     gouts[...] = gout[...].astype(BF)
@@ -419,9 +437,28 @@
     for d in range(1, 4):
         gout_copy(d).start()
 
-    combine(3)
-    send_home(2)
-    send_home(3)
+    for d in (1, 3, 2):
+        kx_copy(d).wait_recv()
+        kc_copy(d).start()
+    for d in range(4):
+        kc_copy(d).wait_recv()
+    absorb(full, True)
+
+    @pl.loop(0, 4)
+    def _(jj):
+        @pl.loop(full * jj // 4, full * (jj + 1) // 4)
+        def _(t):
+            absorb(t, False)
+
+        combine(lax.rem(jj + 1, 4))
+
+        @pl.when(jj >= 1)
+        def _():
+            send_home(jj)
+
+    for h in range(HEADS):
+        ctx_o[:, h * HD : (h + 1) * HD] = (num[h] / den[h, 0:1]).T.astype(BF)
+    send_home(0)
 
     for d in range(1, 8):
         gin_copy(d).wait_recv()
@@ -436,7 +473,7 @@
         total = total + goutr[d].astype(F32)
     gout_o[...] = total
 
-    total = accown[0]
+    total = accown[...]
     for j in (1, 2, 3):
         home_copy(j, sibling).wait_recv()
         total = total + zrb[j - 1].astype(F32)
@@ -473,6 +510,23 @@
             def _():
                 row_copy(j, n).wait_send()
                 remote(retb.at[j, n], outb.at[j, x], os_.at[j, n], orr.at[j, x], sibling).wait_send()
+
+
+def finish_kernel(*refs):
+    half = len(refs) // 2
+    for source, target in zip(refs[:half], refs[half:]):
+        target[...] = source[...]
+
+
+def finish(arrays):
+    vm = pl.BlockSpec(memory_space=pltpu.VMEM)
+    return pl.pallas_call(
+        finish_kernel,
+        out_shape=tuple(jax.ShapeDtypeStruct(a.shape, a.dtype) for a in arrays),
+        in_specs=[vm] * len(arrays),
+        out_specs=(vm,) * len(arrays),
+        name="finish",
+    )(*arrays)
 
 
 def run(queries, keys, values, hidden, cotangent, routes, route_weight, wgu, wd, ain, aout):
@@ -501,18 +555,19 @@
             v((PARTS, LOWR, D), BF),
             v((HALF, RANK, 2 * FF), BF),
             v((HALF, 2 * RANK, 2 * FF), BF),
+            v((NX, BLK, 2 * TOK), BF),
             v((4, NX, BLK, TOK), BF),
             v((4, NX, BLK, TOK), BF),
             v((4, 64, TOK), F32),
-            v((64, D), BF),
-            v((3, 4, 64, D), BF),
+            v((32, 2 * TOK), F32),
+            v((4, 4, 64, D), BF),
             v((4, NX, BLK, D), BF),
             v((4, NX, BLK, D), BF),
-            v((ROWS, D), BF),
-            v((ROWS, D), BF),
-            v((ROWS, D), F32),
-            v((ROWS, 2 * RANK), BF),
-            v((ROWS, 2 * RANK), F32),
+            v((4, ROWS, D), BF),
+            v((4, ROWS, D), BF),
+            v((4, ROWS, D), F32),
+            v((4, ROWS, 2 * RANK), BF),
+            v((4, ROWS, 2 * RANK), F32),
             v((PARTS * LOWR, D), F32),
             v((HALF, RANK, 2 * FF), F32),
             v((4, NX, BLK, D // 2), BF),
@@ -521,8 +576,7 @@
             v((HALF, RANK, 2 * FF), BF),
             v((7, LOWR, D), BF),
             v((3, RANK, 2 * FF), BF),
-            v((TOK, D), F32),
-            v((4, TOK, 512), F32),
+            v((TOK, 512), F32),
             v((4, 4, TOK, 512), BF),
             v((4, 3, TOK, 512), BF),
             v((3, TOK, 512), BF),
@@ -571,10 +625,11 @@
     queries, keys, values, hidden, cotangent, routes, route_weight,
     w_gate_up, w_down, adapter_in, adapter_out,
 ):
-    context, mixed, gin, gout = run(
+    outs = run(
         queries, keys, values, hidden, cotangent, routes.T, route_weight.T,
         w_gate_up[0, 0], w_down[0, 0], adapter_in[0, 0].T, adapter_out[0, 0],
     )
+    context, mixed, gin, gout = finish(outs)
     return (context, mixed, gin.T[None, None], gout[None, None])
 
 

time: 176 us -> 162 us (0.920)
  the two profiles are of different devices: /device:TPU:1 before, /device:TPU:70 now
where the time goes in v4:
time: 162 us; the launch traced here: 160 us
  Pallas kernels  160 us (99%)
    pallas_call x1, Pallas kernels, run(): pl.pallas_call(kernel, out_shape=(jax.ShapeDtypeStruct((TOK, HEADS * HD),...  158 us

profile of v4, /device:TPU:70, one launch (start us, length us, event | category | flops | bytes accessed | tf_op | source)
XLA Modules:
  0.0 160.3 jit_solution(5184872613085938731)
XLA Ops:
  0.6 157.7 %whole.1 = (bf16[128,1024]{1,0:T(8,128)(2,1)}, bf16[128,512]{1,0:T(8,128)(2,1)}, f32[16,2048]{1,0:T(8,128)}, f32[64,384]{1,0:T(8,128)}) custom-call(bf16[128,1024]{1,0:T(8,128)(2,1)} %queries.1, bf16[128,128]{1,0:T(8,128)(2,1)} %keys.1, bf16[128,128]{1,0:T(8,128)(2,1)} %values.1, bf16[128,2048]{1,0:T(8,128)(2,1)} %hid.1, bf16[128,2048]{1,0:T(8,128)(2,1)} %cot.1, ...), custom_call_target="tpu_custom_call" | custom-call | flops 17179869184 | bytes 33554432 | tf_op jit(solution)/shard_map/whole/pallas_call | solution.py:537
  158.3 1.9 %finish.1 = (bf16[128,1024]{1,0:T(8,128)(2,1)}, bf16[128,512]{1,0:T(8,128)(2,1)}, f32[16,2048]{1,0:T(8,128)}, f32[64,384]{1,0:T(8,128)}) custom-call(bf16[128,1024]{1,0:T(8,128)(2,1)} %get-tuple-element.12.refs_0_, bf16[128,512]{1,0:T(8,128)(2,1)} %get-tuple-element.13.refs_1_, f32[16,2048]{1,0:T(8,128)} %get-tuple-element.14.refs_2_, ...), custom_call_target="tpu_custom_call" | custom-call | tf_op jit(solution)/shard_map/finish/pallas_call | solution.py:523

commit v5 on v4

--- a/solution.py
+++ b/solution.py
@@ -437,24 +437,29 @@
     for d in range(1, 4):
         gout_copy(d).start()
 
-    for d in (1, 3, 2):
-        kx_copy(d).wait_recv()
-        kc_copy(d).start()
-    for d in range(4):
-        kc_copy(d).wait_recv()
-    absorb(full, True)
+    def keys_here():
+        for d in (1, 3, 2):
+            kx_copy(d).wait_recv()
+            kc_copy(d).start()
+        for d in range(4):
+            kc_copy(d).wait_recv()
 
     @pl.loop(0, 4)
     def _(jj):
-        @pl.loop(full * jj // 4, full * (jj + 1) // 4)
-        def _(t):
-            absorb(t, False)
-
         combine(lax.rem(jj + 1, 4))
+
+        @pl.when(jj == 0)
+        def _():
+            keys_here()
+            absorb(full, True)
 
         @pl.when(jj >= 1)
         def _():
             send_home(jj)
+
+        @pl.loop(full * jnp.minimum(jj, 3) // 3, full * jnp.minimum(jj + 1, 3) // 3)
+        def _(t):
+            absorb(t, False)
 
     for h in range(HEADS):
         ctx_o[:, h * HD : (h + 1) * HD] = (num[h] / den[h, 0:1]).T.astype(BF)

time: 162 us -> 159 us (0.981)
  Pallas kernels: 160 us -> 157 us
    pallas_call x1, Pallas kernels: 158 us -> 155 us  [run(): pl.pallas_call(kernel, out_shape=(jax.ShapeDtypeStruct((TOK, HEADS * HD),...]
where the time goes in v5:
time: 159 us; the launch traced here: 158 us
  Pallas kernels  157 us (99%)
    pallas_call x1, Pallas kernels, run(): pl.pallas_call(kernel, out_shape=(jax.ShapeDtypeStruct((TOK, HEADS * HD),...  155 us

profile of v5, /device:TPU:70, one launch (start us, length us, event | category | flops | bytes accessed | tf_op | source)
XLA Modules:
  0.0 157.8 jit_solution(357208108239346593)
XLA Ops:
  0.6 155.3 %whole.1 = (bf16[128,1024]{1,0:T(8,128)(2,1)}, bf16[128,512]{1,0:T(8,128)(2,1)}, f32[16,2048]{1,0:T(8,128)}, f32[64,384]{1,0:T(8,128)}) custom-call(bf16[128,1024]{1,0:T(8,128)(2,1)} %queries.1, bf16[128,128]{1,0:T(8,128)(2,1)} %keys.1, bf16[128,128]{1,0:T(8,128)(2,1)} %values.1, bf16[128,2048]{1,0:T(8,128)(2,1)} %hid.1, bf16[128,2048]{1,0:T(8,128)(2,1)} %cot.1, ...), custom_call_target="tpu_custom_call" | custom-call | flops 17179869184 | bytes 33554432 | tf_op jit(solution)/shard_map/whole/pallas_call | solution.py:542
  155.9 1.9 %finish.1 = (bf16[128,1024]{1,0:T(8,128)(2,1)}, bf16[128,512]{1,0:T(8,128)(2,1)}, f32[16,2048]{1,0:T(8,128)}, f32[64,384]{1,0:T(8,128)}) custom-call(bf16[128,1024]{1,0:T(8,128)(2,1)} %get-tuple-element.12.refs_0_, bf16[128,512]{1,0:T(8,128)(2,1)} %get-tuple-element.13.refs_1_, f32[16,2048]{1,0:T(8,128)} %get-tuple-element.14.refs_2_, ...), custom_call_target="tpu_custom_call" | custom-call | tf_op jit(solution)/shard_map/finish/pallas_call | solution.py:528
